TPU v7x, 128 devices: a whole 4x4x4 slice. The times are simulated.
128 devices in a mesh: pair: 8 (over z_hi, x), blk: 16 (over y, z_lo, core).
Axes of the slice: x: 4, y: 4, z: 4 (z_hi: 2, z_lo: 2; z = z_hi * 2 + z_lo), core: 2. Of those that a mesh axis runs over, the one named last changes fastest.
Arguments:
- queries: bfloat16 [8, 2048, 4096], P('pair', 'blk')
- prompt_keys: bfloat16 [8, 4096, 512], P('pair', 'blk')
- prompt_values: bfloat16 [8, 4096, 512], P('pair', 'blk'), may hold values from -6 to 6
- resp_keys: bfloat16 [8, 2048, 512], P('pair', 'blk'), may hold values from -6 to 6
- resp_values: bfloat16 [8, 2048, 512], P('pair', 'blk'), may hold values from -6 to 6
- slot_row: int32 [8, 2048], P('pair', 'blk'), may hold values from -1 to 1023, as said below
- lengths: int32 [8, 2], P('pair'), may hold values from 1 to 768, 1024 in all within a row
- probe: float32 [4096], replicated, may hold values from -6 to 6
Outputs:
- attended: bfloat16 [8, 2048, 4096], P('pair', 'blk')
- loss: float32 [], replicated
Inputs may be any that keep to these rules, and one draw needn't show every extreme that they name: `slot_row`: in each pair every response row 0 to 1023 stands in exactly one slot; the other slots hold -1. On each device the live slots come first. The live slots of a device and of the device half the blk axis away number 2 * 64 together, and some device of each pair has all 128 slots live.
All inputs are finite; a program needn't handle non-finite values.
Results may differ from a plain program's by a relative error of at most 0.024.
Values may be sent and summed in bfloat16 or wider, within the bound.
A program may use at most 128 MiB of HBM per device.

v0:
```python
import jax
import jax.numpy as jnp
from jax import lax
from jax.sharding import PartitionSpec as P

QH = 32
KVH = 4
HD = 128


def update_block(carry, keys, values, key_ids, q4, query_ids, chosen_len):
    running_top, running_total, running_acc = carry
    heads_kv = q4.shape[1]
    head_dim = q4.shape[3]
    count = keys.shape[0]
    keys3 = keys.reshape(count, heads_kv, head_dim)
    values3 = values.reshape(count, heads_kv, head_dim)
    score = jnp.einsum("bkgd,nkd->bkgn", q4, keys3, preferred_element_type=jnp.float32)
    score = score / jnp.sqrt(jnp.float32(head_dim))
    same = (key_ids[None, :] >= chosen_len) == (query_ids[:, None] >= chosen_len)
    earlier = (key_ids[None, :] >= 0) & (key_ids[None, :] <= query_ids[:, None]) & same
    visible = ((key_ids[None, :] == -2) | earlier)[:, None, None, :]
    score = jnp.where(visible, score, jnp.float32(-1e30))
    new_top = jnp.maximum(running_top, jnp.max(score, axis=-1))
    factor = jnp.exp(running_top - new_top)
    raw = jnp.where(visible, jnp.exp(score - new_top[..., None]), jnp.float32(0.0))
    new_total = running_total * factor + jnp.sum(raw, axis=-1)
    product = jnp.einsum(
        "bkgn,nkd->bkgd", raw.astype(jnp.bfloat16), values3, preferred_element_type=jnp.float32
    )
    new_acc = running_acc * factor[..., None] + product
    return (new_top, new_total, new_acc)


def fold_keys(carry, keys, values, key_ids, q4, query_ids, chosen_len):
    count = keys.shape[0]
    size = 512
    steps = count // size
    key_blocks = keys.reshape(steps, size, keys.shape[1])
    value_blocks = values.reshape(steps, size, values.shape[1])
    id_blocks = key_ids.reshape(steps, size)

    def advance(state, block):
        return (update_block(state, block[0], block[1], block[2], q4, query_ids, chosen_len), None)

    carry, _ = lax.scan(advance, carry, (key_blocks, value_blocks, id_blocks))
    return carry


def local(queries, prompt_keys, prompt_values, resp_keys, resp_values, slot_row, lengths, probe):
    groups = QH // KVH
    chosen_len = lengths[0, 0]
    rejected_len = lengths[0, 1]
    slot_ids = slot_row[0]
    query_rows = queries[0]
    rows = query_rows.shape[0]
    q4 = query_rows.reshape(rows, KVH, groups, HD)
    start_state = (
        jnp.full((rows, KVH, groups), -1e30, jnp.float32),
        jnp.zeros((rows, KVH, groups), jnp.float32),
        jnp.zeros((rows, KVH, groups, HD), jnp.float32),
    )
    piece = (
        lax.all_gather(prompt_keys, "blk", axis=1, tiled=True),
        lax.all_gather(prompt_values, "blk", axis=1, tiled=True),
    )
    marker = jnp.full((piece[0].shape[1],), -2, jnp.int32)
    state = fold_keys(start_state, piece[0][0], piece[1][0], marker, q4, slot_ids, chosen_len)
    piece = (
        lax.all_gather(resp_keys, "blk", axis=1, tiled=True),
        lax.all_gather(resp_values, "blk", axis=1, tiled=True),
        lax.all_gather(slot_row, "blk", axis=1, tiled=True),
    )
    state = fold_keys(state, piece[0][0], piece[1][0], piece[2][0], q4, slot_ids, chosen_len)
    final_acc = state[2] / state[1][..., None]
    result = final_acc.reshape(rows, QH * HD)
    result = jnp.where((slot_ids >= 0)[:, None], result, jnp.float32(0.0))
    attended = result.astype(jnp.bfloat16)
    row_score = jnp.dot(attended.astype(jnp.float32), probe, precision=lax.Precision.HIGHEST)
    chosen = (slot_ids >= 0) & (slot_ids < chosen_len)
    rejected = slot_ids >= chosen_len
    part_chosen = jnp.sum(jnp.where(chosen, row_score, jnp.float32(0.0))) / chosen_len.astype(
        jnp.float32
    )
    part_rejected = jnp.sum(jnp.where(rejected, row_score, jnp.float32(0.0))) / rejected_len.astype(
        jnp.float32
    )
    whole_chosen, whole_rejected = lax.psum((part_chosen, part_rejected), "blk")
    term = jax.nn.softplus(-4.0 * (whole_chosen - whole_rejected))
    loss = lax.psum(term, "pair")
    return (attended[None], loss)


def solution(mesh):
    return jax.shard_map(
        local,
        mesh=mesh,
        in_specs=(
            P("pair", "blk", None),
            P("pair", "blk", None),
            P("pair", "blk", None),
            P("pair", "blk", None),
            P("pair", "blk", None),
            P("pair", "blk"),
            P("pair", None),
            P(),
        ),
        out_specs=(P("pair", "blk", None), P()),
        check_vma=False,
    )
```

profile of v0, /device:TPU:1, one launch (start us, length us, event | category | flops | bytes accessed | tf_op | source)
XLA Modules:
  0.0 402.6 jit_solution(16754809779588153820)
XLA Ops:
  10.0 21.7 %all_gather.17 = s32[1,2048]{1,0:T(1,128)S(1)} all-gather(s32[1,128]{1,0:T(1,128)} %param.17), channel_id=1, replica_groups=mesh['pair'=8,'blk'=16] {'blk'}, dimensions={1}, use_global_device_ids=true | all-gather | bytes 8704 | tf_op jit(solution)/shard_map/all_gather | solution.py:72
  38.3 12.5 %all-gather.5.cloned.1.call-done = bf16[1,4096,512]{2,1,0:T(8,128)(2,1)} async-done(((bf16[1,256,512]{2,1,0:T(8,128)(2,1)}), bf16[1,4096,512]{2,1,0:T(8,128)(2,1)}) %all-gather.5.cloned.1.call-update) | async-done | bytes 4194320 | tf_op jit(solution)/shard_map/all_gather | solution.py:64
  50.8 39.2 %all-gather.7.cloned.1.call-done = bf16[1,4096,512]{2,1,0:T(8,128)(2,1)} async-done(((bf16[1,256,512]{2,1,0:T(8,128)(2,1)}), bf16[1,4096,512]{2,1,0:T(8,128)(2,1)}) %all-gather.7.cloned.1.call-update) | async-done | bytes 4194320 | tf_op jit(solution)/shard_map/all_gather | solution.py:65
  90.0 167.5 %while.31 = (s32[]{:T(128)}, f32[128,4,8]{0,2,1:T(8,128)S(1)}, f32[128,4,8]{0,2,1:T(8,128)S(1)}, f32[128,4,8,128]{0,3,2,1:T(8,128)}, bf16[8,512,512]{2,1,0:T(8,1...) while((s32[]{:T(128)}, f32[128,4,8]{0,2,1:T(8,128)S(1)}, ...), condition=%wide.region_3.4_spmd.clone, body=%wide.region_0.3_spmd.clone.sunk | while | flops 1092112384 | bytes 52691108 | solution.py:46
  96.8 5.0 %fusion.57 = f32[128,4,8]{0,2,1:T(8,128)S(1)} fusion(f32[4,512,128,8]{2,1,3,0:T(8,128)} %get-tuple-element.366, f32[128,4,8]{0,2,1:T(8,128)S(1)} %select_maximum_fusion.2), kind=kLoop, calls=%fused_computation.4.clone.1 | loop fusion | flops 6287360 | bytes 8421376 | tf_op jit(solution)/shard_map/while/body/eval_jaxpr/reduce_sum | solution.py:27
  103.9 5.8 %bitcast_add_fusion.5 = f32[128,4,8,128]{0,3,2,1:T(8,128)S(1)} fusion(f32[128,4,8,128]{0,3,2,1:T(8,128)S(1)} %copy-done.2, bf16[512,4,128,1]{0,2,3,1:T(8,128)(2,1)} %bitcast.134, f32[4,512,128,8]{2,1,3,0:T(8,128)} %get-tuple-element.366, f32[128,4,8]{0,2,1:T(8,128)S(1)} %select_maximum_fusion.2, f32[128,4,8]{0,2,1:T(8,128)S(1)} %get-tuple-element.369, ...), kind=kOutput, calls=%fused_computation.8.clone.1 | convolution fusion | flops 544735232 | bytes 13139969 | tf_op jit(solution)/shard_map/while/body/eval_jaxpr/bkgn,nkd->bkgd/dot_general | solution.py:28
  113.2 4.5 %bitcast_reduce_fusion.2 = (f32[128,4,8]{0,2,1:T(8,128)S(1)}, f32[4,512,128,8]{2,1,3,0:T(8,128)}) fusion(bf16[512,4,128,1]{0,2,3,1:T(8,128)(2,1)S(1)} %bitcast.132, bf16[128,4,8,128]{3,0,2,1:T(8,128)(2,1)S(1)} %get-tuple-element.393), kind=kOutput, calls=%fused_computation.1.clone.1 | convolution fusion | flops 541061120 | bytes 9977856 | tf_op jit(solution)/shard_map/while/body/eval_jaxpr/bkgd,nkd->bkgn/dot_general | solution.py:18
  117.8 5.0 %fusion.57 = f32[128,4,8]{0,2,1:T(8,128)S(1)} fusion(f32[4,512,128,8]{2,1,3,0:T(8,128)} %get-tuple-element.366, f32[128,4,8]{0,2,1:T(8,128)S(1)} %select_maximum_fusion.2), kind=kLoop, calls=%fused_computation.4.clone.1 | loop fusion | flops 6287360 | bytes 8421376 | tf_op jit(solution)/shard_map/while/body/eval_jaxpr/reduce_sum | solution.py:27
  124.9 5.7 %bitcast_add_fusion.5 = f32[128,4,8,128]{0,3,2,1:T(8,128)S(1)} fusion(f32[128,4,8,128]{0,3,2,1:T(8,128)S(1)} %copy-done.2, bf16[512,4,128,1]{0,2,3,1:T(8,128)(2,1)} %bitcast.134, f32[4,512,128,8]{2,1,3,0:T(8,128)} %get-tuple-element.366, f32[128,4,8]{0,2,1:T(8,128)S(1)} %select_maximum_fusion.2, f32[128,4,8]{0,2,1:T(8,128)S(1)} %get-tuple-element.369, ...), kind=kOutput, calls=%fused_computation.8.clone.1 | convolution fusion | flops 544735232 | bytes 13139969 | tf_op jit(solution)/shard_map/while/body/eval_jaxpr/bkgn,nkd->bkgd/dot_general | solution.py:28
  134.2 4.5 %bitcast_reduce_fusion.2 = (f32[128,4,8]{0,2,1:T(8,128)S(1)}, f32[4,512,128,8]{2,1,3,0:T(8,128)}) fusion(bf16[512,4,128,1]{0,2,3,1:T(8,128)(2,1)S(1)} %bitcast.132, bf16[128,4,8,128]{3,0,2,1:T(8,128)(2,1)S(1)} %get-tuple-element.393), kind=kOutput, calls=%fused_computation.1.clone.1 | convolution fusion | flops 541061120 | bytes 9977856 | tf_op jit(solution)/shard_map/while/body/eval_jaxpr/bkgd,nkd->bkgn/dot_general | solution.py:18
  138.7 5.0 %fusion.57 = f32[128,4,8]{0,2,1:T(8,128)S(1)} fusion(f32[4,512,128,8]{2,1,3,0:T(8,128)} %get-tuple-element.366, f32[128,4,8]{0,2,1:T(8,128)S(1)} %select_maximum_fusion.2), kind=kLoop, calls=%fused_computation.4.clone.1 | loop fusion | flops 6287360 | bytes 8421376 | tf_op jit(solution)/shard_map/while/body/eval_jaxpr/reduce_sum | solution.py:27
  145.8 5.8 %bitcast_add_fusion.5 = f32[128,4,8,128]{0,3,2,1:T(8,128)S(1)} fusion(f32[128,4,8,128]{0,3,2,1:T(8,128)S(1)} %copy-done.2, bf16[512,4,128,1]{0,2,3,1:T(8,128)(2,1)} %bitcast.134, f32[4,512,128,8]{2,1,3,0:T(8,128)} %get-tuple-element.366, f32[128,4,8]{0,2,1:T(8,128)S(1)} %select_maximum_fusion.2, f32[128,4,8]{0,2,1:T(8,128)S(1)} %get-tuple-element.369, ...), kind=kOutput, calls=%fused_computation.8.clone.1 | convolution fusion | flops 544735232 | bytes 13139969 | tf_op jit(solution)/shard_map/while/body/eval_jaxpr/bkgn,nkd->bkgd/dot_general | solution.py:28
  155.2 4.5 %bitcast_reduce_fusion.2 = (f32[128,4,8]{0,2,1:T(8,128)S(1)}, f32[4,512,128,8]{2,1,3,0:T(8,128)}) fusion(bf16[512,4,128,1]{0,2,3,1:T(8,128)(2,1)S(1)} %bitcast.132, bf16[128,4,8,128]{3,0,2,1:T(8,128)(2,1)S(1)} %get-tuple-element.393), kind=kOutput, calls=%fused_computation.1.clone.1 | convolution fusion | flops 541061120 | bytes 9977856 | tf_op jit(solution)/shard_map/while/body/eval_jaxpr/bkgd,nkd->bkgn/dot_general | solution.py:18
  159.8 5.0 %fusion.57 = f32[128,4,8]{0,2,1:T(8,128)S(1)} fusion(f32[4,512,128,8]{2,1,3,0:T(8,128)} %get-tuple-element.366, f32[128,4,8]{0,2,1:T(8,128)S(1)} %select_maximum_fusion.2), kind=kLoop, calls=%fused_computation.4.clone.1 | loop fusion | flops 6287360 | bytes 8421376 | tf_op jit(solution)/shard_map/while/body/eval_jaxpr/reduce_sum | solution.py:27
  166.8 5.7 %bitcast_add_fusion.5 = f32[128,4,8,128]{0,3,2,1:T(8,128)S(1)} fusion(f32[128,4,8,128]{0,3,2,1:T(8,128)S(1)} %copy-done.2, bf16[512,4,128,1]{0,2,3,1:T(8,128)(2,1)} %bitcast.134, f32[4,512,128,8]{2,1,3,0:T(8,128)} %get-tuple-element.366, f32[128,4,8]{0,2,1:T(8,128)S(1)} %select_maximum_fusion.2, f32[128,4,8]{0,2,1:T(8,128)S(1)} %get-tuple-element.369, ...), kind=kOutput, calls=%fused_computation.8.clone.1 | convolution fusion | flops 544735232 | bytes 13139969 | tf_op jit(solution)/shard_map/while/body/eval_jaxpr/bkgn,nkd->bkgd/dot_general | solution.py:28
  180.7 5.0 %fusion.57 = f32[128,4,8]{0,2,1:T(8,128)S(1)} fusion(f32[4,512,128,8]{2,1,3,0:T(8,128)} %get-tuple-element.366, f32[128,4,8]{0,2,1:T(8,128)S(1)} %select_maximum_fusion.2), kind=kLoop, calls=%fused_computation.4.clone.1 | loop fusion | flops 6287360 | bytes 8421376 | tf_op jit(solution)/shard_map/while/body/eval_jaxpr/reduce_sum | solution.py:27
  187.7 5.7 %bitcast_add_fusion.5 = f32[128,4,8,128]{0,3,2,1:T(8,128)S(1)} fusion(f32[128,4,8,128]{0,3,2,1:T(8,128)S(1)} %copy-done.2, bf16[512,4,128,1]{0,2,3,1:T(8,128)(2,1)} %bitcast.134, f32[4,512,128,8]{2,1,3,0:T(8,128)} %get-tuple-element.366, f32[128,4,8]{0,2,1:T(8,128)S(1)} %select_maximum_fusion.2, f32[128,4,8]{0,2,1:T(8,128)S(1)} %get-tuple-element.369, ...), kind=kOutput, calls=%fused_computation.8.clone.1 | convolution fusion | flops 544735232 | bytes 13139969 | tf_op jit(solution)/shard_map/while/body/eval_jaxpr/bkgn,nkd->bkgd/dot_general | solution.py:28
  197.0 4.5 %bitcast_reduce_fusion.2 = (f32[128,4,8]{0,2,1:T(8,128)S(1)}, f32[4,512,128,8]{2,1,3,0:T(8,128)}) fusion(bf16[512,4,128,1]{0,2,3,1:T(8,128)(2,1)S(1)} %bitcast.132, bf16[128,4,8,128]{3,0,2,1:T(8,128)(2,1)S(1)} %get-tuple-element.393), kind=kOutput, calls=%fused_computation.1.clone.1 | convolution fusion | flops 541061120 | bytes 9977856 | tf_op jit(solution)/shard_map/while/body/eval_jaxpr/bkgd,nkd->bkgn/dot_general | solution.py:18
  201.6 5.0 %fusion.57 = f32[128,4,8]{0,2,1:T(8,128)S(1)} fusion(f32[4,512,128,8]{2,1,3,0:T(8,128)} %get-tuple-element.366, f32[128,4,8]{0,2,1:T(8,128)S(1)} %select_maximum_fusion.2), kind=kLoop, calls=%fused_computation.4.clone.1 | loop fusion | flops 6287360 | bytes 8421376 | tf_op jit(solution)/shard_map/while/body/eval_jaxpr/reduce_sum | solution.py:27
  208.6 5.7 %bitcast_add_fusion.5 = f32[128,4,8,128]{0,3,2,1:T(8,128)S(1)} fusion(f32[128,4,8,128]{0,3,2,1:T(8,128)S(1)} %copy-done.2, bf16[512,4,128,1]{0,2,3,1:T(8,128)(2,1)} %bitcast.134, f32[4,512,128,8]{2,1,3,0:T(8,128)} %get-tuple-element.366, f32[128,4,8]{0,2,1:T(8,128)S(1)} %select_maximum_fusion.2, f32[128,4,8]{0,2,1:T(8,128)S(1)} %get-tuple-element.369, ...), kind=kOutput, calls=%fused_computation.8.clone.1 | convolution fusion | flops 544735232 | bytes 13139969 | tf_op jit(solution)/shard_map/while/body/eval_jaxpr/bkgn,nkd->bkgd/dot_general | solution.py:28
  217.9 4.5 %bitcast_reduce_fusion.2 = (f32[128,4,8]{0,2,1:T(8,128)S(1)}, f32[4,512,128,8]{2,1,3,0:T(8,128)}) fusion(bf16[512,4,128,1]{0,2,3,1:T(8,128)(2,1)S(1)} %bitcast.132, bf16[128,4,8,128]{3,0,2,1:T(8,128)(2,1)S(1)} %get-tuple-element.393), kind=kOutput, calls=%fused_computation.1.clone.1 | convolution fusion | flops 541061120 | bytes 9977856 | tf_op jit(solution)/shard_map/while/body/eval_jaxpr/bkgd,nkd->bkgn/dot_general | solution.py:18
  222.5 5.0 %fusion.57 = f32[128,4,8]{0,2,1:T(8,128)S(1)} fusion(f32[4,512,128,8]{2,1,3,0:T(8,128)} %get-tuple-element.366, f32[128,4,8]{0,2,1:T(8,128)S(1)} %select_maximum_fusion.2), kind=kLoop, calls=%fused_computation.4.clone.1 | loop fusion | flops 6287360 | bytes 8421376 | tf_op jit(solution)/shard_map/while/body/eval_jaxpr/reduce_sum | solution.py:27
  229.5 5.7 %bitcast_add_fusion.5 = f32[128,4,8,128]{0,3,2,1:T(8,128)S(1)} fusion(f32[128,4,8,128]{0,3,2,1:T(8,128)S(1)} %copy-done.2, bf16[512,4,128,1]{0,2,3,1:T(8,128)(2,1)} %bitcast.134, f32[4,512,128,8]{2,1,3,0:T(8,128)} %get-tuple-element.366, f32[128,4,8]{0,2,1:T(8,128)S(1)} %select_maximum_fusion.2, f32[128,4,8]{0,2,1:T(8,128)S(1)} %get-tuple-element.369, ...), kind=kOutput, calls=%fused_computation.8.clone.1 | convolution fusion | flops 544735232 | bytes 13139969 | tf_op jit(solution)/shard_map/while/body/eval_jaxpr/bkgn,nkd->bkgd/dot_general | solution.py:28
  243.4 5.0 %fusion.57 = f32[128,4,8]{0,2,1:T(8,128)S(1)} fusion(f32[4,512,128,8]{2,1,3,0:T(8,128)} %get-tuple-element.366, f32[128,4,8]{0,2,1:T(8,128)S(1)} %select_maximum_fusion.2), kind=kLoop, calls=%fused_computation.4.clone.1 | loop fusion | flops 6287360 | bytes 8421376 | tf_op jit(solution)/shard_map/while/body/eval_jaxpr/reduce_sum | solution.py:27
  250.4 5.7 %bitcast_add_fusion.5 = f32[128,4,8,128]{0,3,2,1:T(8,128)S(1)} fusion(f32[128,4,8,128]{0,3,2,1:T(8,128)S(1)} %copy-done.2, bf16[512,4,128,1]{0,2,3,1:T(8,128)(2,1)} %bitcast.134, f32[4,512,128,8]{2,1,3,0:T(8,128)} %get-tuple-element.366, f32[128,4,8]{0,2,1:T(8,128)S(1)} %select_maximum_fusion.2, f32[128,4,8]{0,2,1:T(8,128)S(1)} %get-tuple-element.369, ...), kind=kOutput, calls=%fused_computation.8.clone.1 | convolution fusion | flops 544735232 | bytes 13139969 | tf_op jit(solution)/shard_map/while/body/eval_jaxpr/bkgn,nkd->bkgd/dot_general | solution.py:28
  257.4 82.2 %while.30 = (s32[]{:T(128)}, f32[128,4,8]{0,2,1:T(8,128)S(1)}, f32[128,4,8]{0,2,1:T(8,128)S(1)}, f32[128,4,8,128]{0,3,2,1:T(8,128)}, s32[4,512]{1,0:T(4,128)S(1)...) while((s32[]{:T(128)}, f32[128,4,8]{0,2,1:T(8,128)S(1)}, ...), condition=%wide.region_7.8_spmd, body=%wide.region_4.7_spmd.sunk | while | flops 1102390912 | bytes 86518216 | solution.py:46
  270.5 6.1 %bitcast_add_fusion.4 = f32[128,4,8,128]{0,3,2,1:T(8,128)S(1)} fusion(f32[128,4,8,128]{0,3,2,1:T(8,128)S(1)} %copy-done.4, bf16[512,4,128,1]{0,2,3,1:T(8,128)(2,1)} %bitcast.135, f32[4,512,128,8]{2,1,3,0:T(8,128)} %copy-done.1, f32[128,4,8]{0,2,1:T(8,128)S(1)} %max.16, pred[128,512]{0,1:T(8,128)(4,1)S(1)} %and_or_fusion.2, ...), kind=kOutput, calls=%fused_computation.24.clone.1 | convolution fusion | flops 548405248 | bytes 13205504 | tf_op jit(solution)/shard_map/while/body/eval_jaxpr/bkgn,nkd->bkgd/dot_general | solution.py:28
  291.1 6.1 %bitcast_add_fusion.4 = f32[128,4,8,128]{0,3,2,1:T(8,128)S(1)} fusion(f32[128,4,8,128]{0,3,2,1:T(8,128)S(1)} %copy-done.4, bf16[512,4,128,1]{0,2,3,1:T(8,128)(2,1)} %bitcast.135, f32[4,512,128,8]{2,1,3,0:T(8,128)} %copy-done.1, f32[128,4,8]{0,2,1:T(8,128)S(1)} %max.16, pred[128,512]{0,1:T(8,128)(4,1)S(1)} %and_or_fusion.2, ...), kind=kOutput, calls=%fused_computation.24.clone.1 | convolution fusion | flops 548405248 | bytes 13205504 | tf_op jit(solution)/shard_map/while/body/eval_jaxpr/bkgn,nkd->bkgd/dot_general | solution.py:28
  311.6 6.1 %bitcast_add_fusion.4 = f32[128,4,8,128]{0,3,2,1:T(8,128)S(1)} fusion(f32[128,4,8,128]{0,3,2,1:T(8,128)S(1)} %copy-done.4, bf16[512,4,128,1]{0,2,3,1:T(8,128)(2,1)} %bitcast.135, f32[4,512,128,8]{2,1,3,0:T(8,128)} %copy-done.1, f32[128,4,8]{0,2,1:T(8,128)S(1)} %max.16, pred[128,512]{0,1:T(8,128)(4,1)S(1)} %and_or_fusion.2, ...), kind=kOutput, calls=%fused_computation.24.clone.1 | convolution fusion | flops 548405248 | bytes 13205504 | tf_op jit(solution)/shard_map/while/body/eval_jaxpr/bkgn,nkd->bkgd/dot_general | solution.py:28
  332.1 6.1 %bitcast_add_fusion.4 = f32[128,4,8,128]{0,3,2,1:T(8,128)S(1)} fusion(f32[128,4,8,128]{0,3,2,1:T(8,128)S(1)} %copy-done.4, bf16[512,4,128,1]{0,2,3,1:T(8,128)(2,1)} %bitcast.135, f32[4,512,128,8]{2,1,3,0:T(8,128)} %copy-done.1, f32[128,4,8]{0,2,1:T(8,128)S(1)} %max.16, pred[128,512]{0,1:T(8,128)(4,1)S(1)} %and_or_fusion.2, ...), kind=kOutput, calls=%fused_computation.24.clone.1 | convolution fusion | flops 548405248 | bytes 13205504 | tf_op jit(solution)/shard_map/while/body/eval_jaxpr/bkgn,nkd->bkgd/dot_general | solution.py:28
  344.8 27.4 %all-reduce = (f32[]{:T(128)}, f32[]{:T(128)}) all-reduce(f32[]{:T(128)S(6)} %div.26, f32[]{:T(128)S(6)} %div.27), channel_id=1, replica_groups=mesh['pair'=8,'blk'=16] {'blk'}, use_global_device_ids=true, to_apply=%region_9.10 | all-reduce | flops 2 | bytes 16 | tf_op jit(solution)/shard_map/psum | solution.py:88
  373.5 20.7 %psum.23 = f32[]{:T(128)} all-reduce(f32[]{:T(128)S(6)} %select_n.37), channel_id=1, replica_groups=mesh['pair'=8,'blk'=16] {'pair'}, use_global_device_ids=true, to_apply=%region_12.13 | all-reduce | flops 1 | bytes 8 | tf_op jit(solution)/shard_map/psum | solution.py:90
  (180 shorter events, 130.0 us)
Async XLA Ops:
  7.2 334.6 %copy-start = (f32[4096]{0:T(1024)S(1)}, f32[4096]{0:T(1024)}, u32[]{:S(2)}) copy-start(f32[4096]{0:T(1024)} %param.19) | copy-start | bytes 49156
  7.2 43.6 %all-gather.5.cloned.1.call-start = ((), (), s32[]{:S(2)}) async-start(), calls=%async_computation | async-start | bytes 4456448 | tf_op jit(solution)/shard_map/all_gather | solution.py:64
  7.9 82.1 %all-gather.7.cloned.1.call-start = ((), (), s32[]{:S(2)}) async-start(), calls=%async_computation.1 | async-start | bytes 4456448 | tf_op jit(solution)/shard_map/all_gather | solution.py:65
  8.7 248.8 %all-gather.9.cloned.1.call-start = ((), (), s32[]{:S(2)}) async-start(), calls=%async_computation.2 | async-start | bytes 2228224 | tf_op jit(solution)/shard_map/all_gather | solution.py:70
  9.4 248.0 %all-gather.11.cloned.1.call-start = ((), (), s32[]{:S(2)}) async-start(), calls=%async_computation.3 | async-start | bytes 2228224 | tf_op jit(solution)/shard_map/all_gather | solution.py:71
  90.0 167.5 %copy-start.6 = (s32[1,128]{1,0:T(1,128)S(1)}, s32[1,128]{1,0:T(1,128)}, u32[]{:S(2)}) copy-start(s32[1,128]{1,0:T(1,128)} %param.17) | copy-start | bytes 1540
  96.8 7.1 %copy-start.2 = (f32[128,4,8,128]{0,3,2,1:T(8,128)S(1)}, f32[128,4,8,128]{0,3,2,1:T(8,128)}, u32[]{:S(2)}) copy-start(f32[128,4,8,128]{0,3,2,1:T(8,128)} %get-tuple-element.382) | copy-start | bytes 6291460 | tf_op jit(solution)/shard_map/while
  109.6 1.3 copy-start.3
  117.8 7.1 %copy-start.2 = (f32[128,4,8,128]{0,3,2,1:T(8,128)S(1)}, f32[128,4,8,128]{0,3,2,1:T(8,128)}, u32[]{:S(2)}) copy-start(f32[128,4,8,128]{0,3,2,1:T(8,128)} %get-tuple-element.382) | copy-start | bytes 6291460 | tf_op jit(solution)/shard_map/while
  130.6 1.3 copy-start.3
  138.7 7.1 %copy-start.2 = (f32[128,4,8,128]{0,3,2,1:T(8,128)S(1)}, f32[128,4,8,128]{0,3,2,1:T(8,128)}, u32[]{:S(2)}) copy-start(f32[128,4,8,128]{0,3,2,1:T(8,128)} %get-tuple-element.382) | copy-start | bytes 6291460 | tf_op jit(solution)/shard_map/while
  151.6 1.3 copy-start.3
  159.8 7.1 %copy-start.2 = (f32[128,4,8,128]{0,3,2,1:T(8,128)S(1)}, f32[128,4,8,128]{0,3,2,1:T(8,128)}, u32[]{:S(2)}) copy-start(f32[128,4,8,128]{0,3,2,1:T(8,128)} %get-tuple-element.382) | copy-start | bytes 6291460 | tf_op jit(solution)/shard_map/while
  172.5 1.3 copy-start.3
  180.7 7.1 %copy-start.2 = (f32[128,4,8,128]{0,3,2,1:T(8,128)S(1)}, f32[128,4,8,128]{0,3,2,1:T(8,128)}, u32[]{:S(2)}) copy-start(f32[128,4,8,128]{0,3,2,1:T(8,128)} %get-tuple-element.382) | copy-start | bytes 6291460 | tf_op jit(solution)/shard_map/while
  193.4 1.3 copy-start.3
  201.6 7.1 %copy-start.2 = (f32[128,4,8,128]{0,3,2,1:T(8,128)S(1)}, f32[128,4,8,128]{0,3,2,1:T(8,128)}, u32[]{:S(2)}) copy-start(f32[128,4,8,128]{0,3,2,1:T(8,128)} %get-tuple-element.382) | copy-start | bytes 6291460 | tf_op jit(solution)/shard_map/while
  214.3 1.3 copy-start.3
  222.5 7.1 %copy-start.2 = (f32[128,4,8,128]{0,3,2,1:T(8,128)S(1)}, f32[128,4,8,128]{0,3,2,1:T(8,128)}, u32[]{:S(2)}) copy-start(f32[128,4,8,128]{0,3,2,1:T(8,128)} %get-tuple-element.382) | copy-start | bytes 6291460 | tf_op jit(solution)/shard_map/while
  235.2 1.3 copy-start.3
  243.4 7.1 %copy-start.2 = (f32[128,4,8,128]{0,3,2,1:T(8,128)S(1)}, f32[128,4,8,128]{0,3,2,1:T(8,128)}, u32[]{:S(2)}) copy-start(f32[128,4,8,128]{0,3,2,1:T(8,128)} %get-tuple-element.382) | copy-start | bytes 6291460 | tf_op jit(solution)/shard_map/while
  256.1 1.3 copy-start.3
  262.7 3.5 copy-start.1
  262.7 7.8 %copy-start.4 = (f32[128,4,8,128]{0,3,2,1:T(8,128)S(1)}, f32[128,4,8,128]{0,3,2,1:T(8,128)}, u32[]{:S(2)}) copy-start(f32[128,4,8,128]{0,3,2,1:T(8,128)} %get-tuple-element.411) | copy-start | bytes 6291460 | tf_op jit(solution)/shard_map/while
  276.7 1.3 copy-start.5
  283.2 3.5 copy-start.1
  283.2 7.8 %copy-start.4 = (f32[128,4,8,128]{0,3,2,1:T(8,128)S(1)}, f32[128,4,8,128]{0,3,2,1:T(8,128)}, u32[]{:S(2)}) copy-start(f32[128,4,8,128]{0,3,2,1:T(8,128)} %get-tuple-element.411) | copy-start | bytes 6291460 | tf_op jit(solution)/shard_map/while
  297.2 1.3 copy-start.5
  303.8 3.5 copy-start.1
  303.8 7.8 %copy-start.4 = (f32[128,4,8,128]{0,3,2,1:T(8,128)S(1)}, f32[128,4,8,128]{0,3,2,1:T(8,128)}, u32[]{:S(2)}) copy-start(f32[128,4,8,128]{0,3,2,1:T(8,128)} %get-tuple-element.411) | copy-start | bytes 6291460 | tf_op jit(solution)/shard_map/while
  324.3 3.5 copy-start.1
  324.3 7.8 %copy-start.4 = (f32[128,4,8,128]{0,3,2,1:T(8,128)S(1)}, f32[128,4,8,128]{0,3,2,1:T(8,128)}, u32[]{:S(2)}) copy-start(f32[128,4,8,128]{0,3,2,1:T(8,128)} %get-tuple-element.411) | copy-start | bytes 6291460 | tf_op jit(solution)/shard_map/while
  (2 other events, 2.7 us)
Sparse Core Ops, SparseCore 0:
  9.7 41.0 all-gather.4
  52.5 37.4 all-gather.6
  91.7 33.8 all-gather.8
  127.2 34.0 all-gather.10
where the time goes:
time: 409 us; the launch traced here: 403 us
  matrix products  114 us (28%)
  local copies, waits for them, and re-layouts  86.7 us (21%)
  blocking collectives  69.7 us (17%)
  other arithmetic  59.3 us (14%)
  waiting for transfers between devices  54.2 us (13%)
  between operations  17.8 us (4%)
    dot_general x12, matrix products, update_block(): jnp.einsum('bkgn,nkd->bkgd', raw.astype(jnp.bfloat16), values3, preferred...  70.2 us
    dynamic_slice x36, local copies, waits for them, and re-layouts, fold_keys(): carry, _ = lax.scan(advance, carry, (key_blocks, value_blocks, id_blocks))  52.3 us
    reduce_sum x12, other arithmetic, update_block(): new_total = running_total * factor + jnp.sum(raw, axis=-1)  48.3 us
    dot_general x12, matrix products, update_block(): jnp.einsum('bkgd,nkd->bkgn', q4, keys3, preferred_element_type=jnp.float32)  42.1 us
    all_gather x1, waiting for transfers between devices, local(): lax.all_gather(prompt_values, 'blk', axis=1, tiled=True)  39.2 us
    while x68, local copies, waits for them, and re-layouts  29.8 us
    psum x1, blocking collectives, local(): whole_chosen, whole_rejected = lax.psum((part_chosen, part_rejected), 'blk')  27.4 us
    all_gather x1, blocking collectives, local(): lax.all_gather(slot_row, 'blk', axis=1, tiled=True)  21.7 us
  transfers between devices with their start and end apart: 4, of which 2 were waited for; matrix products, arithmetic and copies ran while one was open for 40% of the time, Pallas kernels for 0%

commit v1 on v0

v1 whole, which is shorter than its diff:
```python
import functools

import jax
import jax.numpy as jnp
from jax import lax
from jax.experimental import pallas as pl
from jax.experimental.pallas import tpu as pltpu
from jax.sharding import PartitionSpec as P

QH = 32
KVH = 4
HD = 128
GROUP = QH // KVH
SLOT = 128
PKEYS = 256
NY = 4
NBLK = 16
WIDE = GROUP * HD
SCALE = 1.4426950408889634 / HD**0.5
MESH = pl.DeviceIdType.MESH
BF = jnp.bfloat16
F32 = jnp.float32
LOW = -1e30
HIGH = 3e38


def dot_t(a, b):
    return lax.dot_general(a, b, (((1,), (1,)), ((), ())), preferred_element_type=F32)


def dot(a, b):
    return jnp.dot(a, b, preferred_element_type=F32)


def kernel(
    n_pair,
    q_hbm, kp_hbm, vp_hbm, kr_hbm, vr_hbm, slot_ref, len_ref, probe_ref,
    att_ref, loss_ref,
    kv, idb, qin, qs, krm, vrm, bias, qid, top, acc, score, osend, oin, part, term,
    local_sem, kv_send, kv_recv, z_send, z_recv, c_send, c_recv, zc_send, zc_recv,
    id_send, id_recv, q_send, q_recv, o_send, o_recv, p_send, p_recv, t_send, t_recv,
):
    pair = lax.axis_index("pair")
    blk = lax.axis_index("blk")
    y, z, c = blk // 4, (blk // 2) % 2, blk % 2

    def device(dy, dz, dc):
        return (pair, ((y + dy) % NY) * 4 + ((z + dz) % 2) * 2 + (c + dc) % 2)

    others = [(dy, dz, dc) for dz in range(2) for dc in range(2) for dy in range(NY)][1:]

    def remote(src, dst, send, recv, target):
        return pltpu.make_async_remote_copy(
            src_ref=src, dst_ref=dst, send_sem=send, recv_sem=recv,
            device_id=target, device_id_type=MESH,
        )

    def columns(head, width):
        return pl.ds(pl.multiple_of(head * width, width), width)

    def kv_parts(head, slot):
        cols = columns(head, HD)
        return (
            (kp_hbm.at[:, cols], kv.at[slot, pl.ds(0, PKEYS)]),
            (vp_hbm.at[:, cols], kv.at[slot, pl.ds(PKEYS, PKEYS)]),
            (kr_hbm.at[:, cols], kv.at[slot, pl.ds(2 * PKEYS, SLOT)]),
            (vr_hbm.at[:, cols], kv.at[slot, pl.ds(2 * PKEYS + SLOT, SLOT)]),
        )

    own = [pltpu.make_async_copy(s, d, local_sem.at[i]) for i, (s, d) in enumerate(kv_parts(y, y))]
    own_q = pltpu.make_async_copy(q_hbm.at[:, columns(y, WIDE)], qin.at[y], local_sem.at[4])
    for copy in own:
        copy.start()
    own_q.start()
    idb[y] = jnp.broadcast_to(slot_ref[...], (8, SLOT))

    barrier = pltpu.get_barrier_semaphore()
    for dy, dz, dc in others:
        pl.semaphore_signal(barrier, inc=1, device_id=device(dy, dz, dc), device_id_type=MESH)
    for d in range(1, n_pair):
        pl.semaphore_signal(
            barrier, inc=1, device_id=((pair + d) % n_pair, blk), device_id_type=MESH
        )
    pl.semaphore_wait(barrier, NBLK - 1 + n_pair - 1)

    kv_copies = {}
    for dy in (1, 3, 2):
        to = device(dy, 0, 0)
        for s, d in kv_parts((y + dy) % NY, y):
            remote(s, d, kv_send.at[dy], kv_recv.at[dy], to).start()
        kv_copies[dy] = remote(kv.at[y], kv.at[y], kv_send.at[dy], kv_recv.at[dy], to)
    id_copies = []
    for i, (dy, dz, dc) in enumerate(others):
        copy = remote(
            idb.at[y], idb.at[dz * 8 + dc * 4 + y], id_send.at[i], id_recv.at[i], device(dy, dz, dc)
        )
        copy.start()
        id_copies.append(copy)
    q_copies = {}
    for dy in (2, 1, 3):
        q_copies[dy] = remote(
            q_hbm.at[:, columns((y + dy) % NY, WIDE)], qin.at[y],
            q_send.at[dy], q_recv.at[dy], device(dy, 0, 0),
        )

    z_copies, c_copies, zc_copies = {}, {}, {}

    def forward(dy):
        at = (y - dy + NY) % NY
        z_copies[dy] = remote(
            kv.at[at], kv.at[8 + at], z_send.at[dy], z_recv.at[dy], device(0, 1, 0)
        )
        c_copies[dy] = remote(
            kv.at[at], kv.at[4 + at], c_send.at[dy], c_recv.at[dy], device(0, 0, 1)
        )
        z_copies[dy].start()
        c_copies[dy].start()

    for copy in own:
        copy.wait()
    forward(0)

    for copy in id_copies:
        copy.wait_recv()
    rows = lax.broadcasted_iota(jnp.int32, (SLOT, SLOT), 0)
    cols = lax.broadcasted_iota(jnp.int32, (SLOT, SLOT), 1)
    same = rows == cols
    turned = rows + cols == SLOT - 1
    turn = jnp.where(turned, 1.0, 0.0).astype(BF)

    def column_of(row, where):
        return jnp.sum(jnp.where(where, row, 0.0), axis=1, keepdims=True)

    def merged_ids(first, second):
        col = column_of(idb[first][:1].astype(F32), same)
        back = column_of(idb[second][:1].astype(F32), turned)
        return col, jnp.where(col >= 0.0, col, back)

    def key_ids(first, second):
        live, ids = merged_ids(first, second)
        return live, jnp.sum(jnp.where(same, ids, 0.0), axis=0, keepdims=True)

    lives, id_rows = [], []
    for g in range(4):
        for j in range(2):
            live, row = key_ids(4 * g + j, 4 * g + j + 2)
            lives.append(live)
            id_rows.append(row)
    chosen_len = len_ref[:1, :1].astype(F32)
    rejected_len = len_ref[:1, 1:2].astype(F32)
    firsts = (y % 2, (y + 1) % 2)
    for n in range(2):
        _, ids = merged_ids(firsts[n], firsts[n] + 2)
        lowest = jnp.where(ids >= chosen_len, chosen_len, 0.0)
        qid[n] = jnp.broadcast_to(ids, (SLOT, HD))
        for m in range(8):
            visible = (id_rows[m] <= ids) & (id_rows[m] >= lowest)
            bias[n, :, m * SLOT : (m + 1) * SLOT] = jnp.where(visible, HIGH, LOW)

    for dy in (1, 3):
        kv_copies[dy].wait_recv()
        forward(dy)
    q_copies[2].start()
    kv_copies[2].wait_recv()
    forward(2)
    q_copies[1].start()
    q_copies[3].start()

    def load_queries(n):
        first = firsts[n]
        live = qid[n]
        col = column_of(idb[first][:1].astype(F32), same)
        back = dot(turn, qin[first + 2])
        del live
        for h in range(GROUP):
            at = slice(h * HD, (h + 1) * HD)
            x = jnp.where(col >= 0.0, qin[first, :, at].astype(F32), back[:, at]) * SCALE
            high = x.astype(BF)
            qs[n, at, :HD] = high
            qs[n, at, HD:] = (x - high.astype(F32)).astype(BF)

    def twice(k):
        return jnp.concatenate([k, k], axis=1)

    def with_ones(v):
        return jnp.concatenate([v, jnp.ones_like(v)], axis=1)

    def prompt(group, at):
        return kv[pl.ds(group * 4, 8), pl.ds(at, PKEYS), :].reshape(8 * PKEYS, HD)

    HALF = 2 * HD

    def scores(n, i, keys):
        q = [qs[n, pl.ds(i * 2 * HALF + j * HALF, HALF), :] for j in range(2)]
        return [[dot_t(x, k) for k in keys] for x in q]

    def masked(n, s):
        limit = bias[n]
        return jnp.minimum(s, jnp.concatenate([limit, limit], axis=0))

    def highest(parts):
        tops = [jnp.max(s, axis=1, keepdims=True) for s in parts]
        return functools.reduce(jnp.maximum, tops)

    def weigh(parts, high, values):
        return sum(
            dot(jnp.exp2(s - high).astype(BF), v) for s, v in zip(parts, values)
        )

    def finish(n, i, j, result):
        out = (result[:, :HD] / result[:, HD:]).astype(BF)
        for h in range(2):
            head = 2 * j + h
            x = out[h * HD : (h + 1) * HD]
            osend[n, i, :, head * HD : (head + 1) * HD] = x
            weights = probe_ref[pl.ds(y * GROUP + i * 4 + head, 1), :]
            score[n] = score[n] + x.astype(F32) * weights

    score[...] = jnp.zeros_like(score)

    own_q.wait()
    q_copies[2].wait_recv()
    load_queries(0)
    for dy in range(NY):
        c_copies[dy].wait_recv()

    def near(i, carry):
        keys, values = [twice(prompt(0, 0))], [with_ones(prompt(0, PKEYS))]
        for j, parts in enumerate(scores(0, i, keys)):
            high = highest(parts)
            at = pl.ds(i * 2 * HALF + j * HALF, HALF)
            top[at, :] = jnp.broadcast_to(high, (HALF, HD))
            acc[at, :] = weigh(parts, high, values)
        return carry

    lax.fori_loop(0, 2, near, 0)

    for dy in (0, 1, 3, 2):
        at = 8 + (y - dy + NY) % NY
        z_copies[dy].wait_recv()
        zc_copies[dy] = remote(
            kv.at[at], kv.at[4 + at], zc_send.at[dy], zc_recv.at[dy], device(0, 0, 1)
        )
        zc_copies[dy].start()
    for dy in range(NY):
        zc_copies[dy].wait_recv()

    for g in range(4):
        for j in range(2):
            m = 2 * g + j
            live = lives[m] >= 0.0
            tail = slice(2 * PKEYS, 2 * PKEYS + 2 * SLOT)
            one = kv[4 * g + j, tail, :].astype(F32)
            two = kv[4 * g + j + 2, tail, :]
            at = slice(m * SLOT, (m + 1) * SLOT)
            krm[at, :] = jnp.where(live, one[:SLOT], dot(turn, two[:SLOT])).astype(BF)
            vrm[at, :] = jnp.where(live, one[SLOT:], dot(turn, two[SLOT:])).astype(BF)

    def out_copies(n, i):
        copies = []
        for k, dy in enumerate(((2,), (1, 3))[n]):
            copies.append(
                remote(
                    osend.at[n, i], oin.at[y, i],
                    o_send.at[dy, i], o_recv.at[dy, i], device(dy, 0, 0),
                )
            )
        return copies

    def far(i, carry):
        keys = [twice(prompt(2, 0)), twice(krm[...])]
        values = [with_ones(prompt(2, PKEYS)), with_ones(vrm[...])]
        for j, parts in enumerate(scores(0, i, keys)):
            parts = [parts[0], masked(0, parts[1])]
            at = pl.ds(i * 2 * HALF + j * HALF, HALF)
            before = top[at, :]
            high = jnp.maximum(before, highest(parts))
            factor = jnp.exp2(before - high)
            result = weigh(parts, high[:, :1], values)
            total = acc[at, :] * jnp.concatenate([factor, factor], axis=1) + result
            finish(0, i, j, total)
        for copy in out_copies(0, i):
            copy.start()
        return carry

    lax.fori_loop(0, 2, far, 0)

    q_copies[1].wait_recv()
    q_copies[3].wait_recv()
    load_queries(1)

    def whole(i, carry):
        keys = [twice(prompt(0, 0)), twice(prompt(2, 0)), twice(krm[...])]
        values = [with_ones(prompt(0, PKEYS)), with_ones(prompt(2, PKEYS)), with_ones(vrm[...])]
        for j, parts in enumerate(scores(1, i, keys)):
            parts = [parts[0], parts[1], masked(1, parts[2])]
            finish(1, i, j, weigh(parts, highest(parts), values))
        for copy in out_copies(1, i):
            copy.start()
        return carry

    lax.fori_loop(0, 2, whole, 0)

    chosen = jnp.zeros((1, 1), F32)
    rejected = jnp.zeros((1, 1), F32)

    def total_of(x):
        return jnp.sum(jnp.sum(x, axis=1, keepdims=True), axis=0, keepdims=True)

    for n in range(2):
        first = qid[n] < chosen_len
        chosen = chosen + total_of(jnp.where(first, score[n], 0.0))
        rejected = rejected + total_of(jnp.where(first, 0.0, score[n]))
    lane = lax.broadcasted_iota(jnp.int32, (8, HD), 1)
    part[blk] = jnp.where(lane == 0, chosen, jnp.where(lane == 1, rejected, 0.0))
    p_copies = []
    for i, (dy, dz, dc) in enumerate(others):
        copy = remote(
            part.at[blk], part.at[blk], p_send.at[i], p_recv.at[i], device(dy, dz, dc)
        )
        copy.start()
        p_copies.append(copy)
    for copy in p_copies:
        copy.wait_recv()
    sums = part[0]
    for i in range(1, NBLK):
        sums = sums + part[i]
    margin = sums[:1, :1] / chosen_len - sums[:1, 1:2] / rejected_len
    x = -4.0 * margin
    value = jnp.maximum(x, 0.0) + jnp.log1p(jnp.exp(-jnp.abs(x)))
    term[pair] = jnp.broadcast_to(value, (8, HD))
    t_copies = []
    for d in range(1, n_pair):
        copy = remote(
            term.at[pair], term.at[pair], t_send.at[d - 1], t_recv.at[d - 1],
            ((pair + d) % n_pair, blk),
        )
        copy.start()
        t_copies.append(copy)

    live = column_of(idb[y][:1].astype(F32), same) >= 0.0
    back = y >= 2
    take = jnp.where(back, SLOT - 1 - rows, rows) == cols
    place = jnp.where(live & take, 1.0, 0.0).astype(BF)

    def put(head, i, x):
        at = pl.ds(pl.multiple_of(head * WIDE + i * (WIDE // 2), WIDE // 2), WIDE // 2)
        att_ref[:, at] = dot(place, x).astype(BF)

    for i in range(2):
        put(y, i, osend[0, i])
    for n, dys in enumerate(((2,), (1, 3))):
        for i in range(2):
            for copy, dy in zip(out_copies(n, i), dys):
                copy.wait_recv()
                source = (y - dy + NY) % NY
                put(source, i, oin[source, i])

    for copy in t_copies:
        copy.wait_recv()
    loss = term[0]
    for i in range(1, n_pair):
        loss = loss + term[i]
    loss_ref[...] = loss[:1, :1]

    for dy in (1, 2, 3):
        kv_copies[dy].wait_send()
        q_copies[dy].wait_send()
    for dy in range(NY):
        z_copies[dy].wait_send()
        c_copies[dy].wait_send()
        zc_copies[dy].wait_send()
    for n in range(2):
        for i in range(2):
            for copy in out_copies(n, i):
                copy.wait_send()
    for copy in id_copies + p_copies + t_copies:
        copy.wait_send()


def local(n_pair, queries, prompt_keys, prompt_values, resp_keys, resp_values, slot_row, lengths, probe):
    vmem = pl.BlockSpec(memory_space=pltpu.VMEM)
    anywhere = pl.BlockSpec(memory_space=pl.ANY)
    sems = pltpu.SemaphoreType.DMA
    attended, loss = pl.pallas_call(
        functools.partial(kernel, n_pair),
        out_shape=(
            jax.ShapeDtypeStruct((SLOT, QH * HD), BF),
            jax.ShapeDtypeStruct((1, 1), F32),
        ),
        in_specs=[anywhere] * 5 + [vmem] * 3,
        out_specs=(vmem, vmem),
        scratch_shapes=[
            pltpu.VMEM((NBLK, 2 * PKEYS + 2 * SLOT, HD), BF),
            pltpu.VMEM((NBLK, 8, SLOT), jnp.int32),
            pltpu.VMEM((NY, SLOT, WIDE), BF),
            pltpu.VMEM((2, WIDE, 2 * HD), BF),
            pltpu.VMEM((8 * SLOT, HD), BF),
            pltpu.VMEM((8 * SLOT, HD), BF),
            pltpu.VMEM((2, SLOT, 8 * SLOT), F32),
            pltpu.VMEM((2, SLOT, HD), F32),
            pltpu.VMEM((WIDE, HD), F32),
            pltpu.VMEM((WIDE, 2 * HD), F32),
            pltpu.VMEM((2, SLOT, HD), F32),
            pltpu.VMEM((2, 2, SLOT, WIDE // 2), BF),
            pltpu.VMEM((NY, 2, SLOT, WIDE // 2), BF),
            pltpu.VMEM((NBLK, 8, HD), F32),
            pltpu.VMEM((n_pair, 8, HD), F32),
            sems((5,)),
            sems((NY,)), sems((NY,)),
            sems((NY,)), sems((NY,)),
            sems((NY,)), sems((NY,)),
            sems((NY,)), sems((NY,)),
            sems((NBLK - 1,)), sems((NBLK - 1,)),
            sems((NY,)), sems((NY,)),
            sems((NY, 2)), sems((NY, 2)),
            sems((NBLK - 1,)), sems((NBLK - 1,)),
            sems((8,)), sems((8,)),
        ],
        compiler_params=pltpu.CompilerParams(
            collective_id=0, has_side_effects=True, vmem_limit_bytes=56 * 2**20
        ),
        cost_estimate=pl.CostEstimate(
            flops=5_400_000_000, bytes_accessed=4_000_000, transcendentals=10_500_000
        ),
    )(
        queries[0], prompt_keys[0], prompt_values[0], resp_keys[0], resp_values[0],
        slot_row, lengths, probe.reshape(QH, HD),
    )
    return attended[None], loss[0, 0]


def solution(mesh):
    return jax.shard_map(
        functools.partial(local, mesh.shape["pair"]),
        mesh=mesh,
        in_specs=(
            P("pair", "blk", None),
            P("pair", "blk", None),
            P("pair", "blk", None),
            P("pair", "blk", None),
            P("pair", "blk", None),
            P("pair", "blk"),
            P("pair", None),
            P(),
        ),
        out_specs=(P("pair", "blk", None), P()),
        check_vma=False,
    )
```

time: 409 us -> 68.5 us (0.17); the launches traced: 403 us -> 68.1 us
  matrix products: 114 us -> 0 us
  local copies, waits for them, and re-layouts: 86.7 us -> 2.29 us
  blocking collectives: 69.7 us -> 0 us
  Pallas kernels: 0 us -> 63.5 us
  other arithmetic: 59.3 us -> 0 us
  waiting for transfers between devices: 54.2 us -> 0 us
  between operations: 17.8 us -> 2.33 us
    dot_general x25 -> x0, matrix products: 114 us -> none  [the longest x12 70.2 us: update_block(): jnp.einsum('bkgn,nkd->bkgd', raw.astype(jnp.bfloat16), values3, preferred...]
    pallas_call x0 -> x1, Pallas kernels: none -> 63.5 us  [local(): pl.pallas_call(functools.partial(kernel, n_pair), out_shape=(jax.ShapeDty...]
    dynamic_slice x36 -> x0, local copies, waits for them, and re-layouts: 52.3 us -> none  [fold_keys(): carry, _ = lax.scan(advance, carry, (key_blocks, value_blocks, id_blocks))]
    all_gather x4 -> x0, waiting for transfers between devices: 51.6 us -> none  [the longest x1 39.2 us: local(): lax.all_gather(prompt_values, 'blk', axis=1, tiled=True)]
    reduce_sum x12 -> x0, other arithmetic: 48.3 us -> none  [update_block(): new_total = running_total * factor + jnp.sum(raw, axis=-1)]
    psum x2 -> x0, blocking collectives: 48.1 us -> none  [the longest x1 27.4 us: local(): whole_chosen, whole_rejected = lax.psum((part_chosen, part_rejected), 'blk')]
    while x68 -> x0, local copies, waits for them, and re-layouts: 29.8 us -> none
    all_gather x1 -> x0, blocking collectives: 21.7 us -> none  [local(): lax.all_gather(slot_row, 'blk', axis=1, tiled=True)]
  transfers between devices with their start and end apart: 4 -> 0, of which waited for: 2 -> 0; matrix products, arithmetic and copies ran while one was open for 40% -> 0% of each run, Pallas kernels for 0% -> 0%
where the time goes in v1:
time: 68.5 us; the launch traced here: 68.1 us
  Pallas kernels  63.5 us (93%)
  between operations  2.33 us (3%)
  local copies, waits for them, and re-layouts  2.29 us (3%)
    pallas_call x1, Pallas kernels, local(): pl.pallas_call(functools.partial(kernel, n_pair), out_shape=(jax.ShapeDty...  63.5 us
    unnamed x1, local copies, waits for them, and re-layouts  2.29 us

profile of v1, /device:TPU:1, one launch (start us, length us, event | category | flops | bytes accessed | tf_op | source)
XLA Modules:
  0.0 68.1 jit_solution(2261986860793083302)
XLA Ops:
  0.6 63.5 %shard_map.95 = (bf16[128,4096]{1,0:T(8,128)(2,1)}, f32[1,1]{1,0:T(1,128)}) custom-call(bf16[128,4096]{1,0:T(8,128)(2,1)} %bitcast.9, bf16[256,512]{1,0:T(8,128)(2,1)} %bitcast.10, bf16[256,512]{1,0:T(8,128)(2,1)} %bitcast.11, bf16[128,512]{1,0:T(8,128)(2,1)} %bitcast.12, bf16[128,512]{1,0:T(8,128)(2,1)} %bitcast.13, s32[1,128]{1,0:T(1,128)} %slot_ref.1, ...), custom_call_target="tpu_custom_call" | custom-call | flops 5400000000 | bytes 4000000 | tf_op jit(solution)/shard_map/pallas_call | solution.py:385
  64.1 2.3 %copy.12 = bf16[1,128,4096]{2,1,0:T(8,128)(2,1)} copy(bf16[1,128,4096]{2,1,0:T(8,128)(2,1)} %bitcast.8) | data formatting | bytes 2097152

commit v2 on v1

--- a/solution.py
+++ b/solution.py
@@ -15,6 +15,9 @@
 PKEYS = 256
 NY = 4
 NBLK = 16
+PAIRS = 8
+IDS = 16
+BLOCK = 2 * PKEYS + 2 * SLOT
 WIDE = GROUP * HD
 SCALE = 1.4426950408889634 / HD**0.5
 MESH = pl.DeviceIdType.MESH
@@ -33,21 +36,29 @@
 
 
 def kernel(
-    n_pair,
     q_hbm, kp_hbm, vp_hbm, kr_hbm, vr_hbm, slot_ref, len_ref, probe_ref,
     att_ref, loss_ref,
-    kv, idb, qin, qs, krm, vrm, bias, qid, top, acc, score, osend, oin, part, term,
+    kv, own_ids, qin, qs, krm, vrm, bias, qid, top, acc, score, osend, oin, part, whole_sums,
     local_sem, kv_send, kv_recv, z_send, z_recv, c_send, c_recv, zc_send, zc_recv,
-    id_send, id_recv, q_send, q_recv, o_send, o_recv, p_send, p_recv, t_send, t_recv,
+    q_send, q_recv, o_send, o_recv, p_send, p_recv, t_send, t_recv,
 ):
     pair = lax.axis_index("pair")
     blk = lax.axis_index("blk")
     y, z, c = blk // 4, (blk // 2) % 2, blk % 2
+    x, z4 = pair % 4, pair // 4 * 2 + z
 
     def device(dy, dz, dc):
         return (pair, ((y + dy) % NY) * 4 + ((z + dz) % 2) * 2 + (c + dc) % 2)
 
-    others = [(dy, dz, dc) for dz in range(2) for dc in range(2) for dy in range(NY)][1:]
+    def across(dx, dy, dz4, dc):
+        to = (z4 + dz4) % 4
+        return (
+            to // 2 * 4 + (x + dx) % 4,
+            ((y + dy) % NY) * 4 + (to % 2) * 2 + (c + dc) % 2,
+        )
+
+    column = [(0, 0, dz4, dc) for dz4 in range(4) for dc in range(2)][1:]
+    plane = [(dx, dy, 0, 0) for dx in range(4) for dy in range(NY)][1:]
 
     def remote(src, dst, send, recv, target):
         return pltpu.make_async_remote_copy(
@@ -72,36 +83,31 @@
     for copy in own:
         copy.start()
     own_q.start()
-    idb[y] = jnp.broadcast_to(slot_ref[...], (8, SLOT))
+    shifted = jnp.broadcast_to(slot_ref[...] + 32, (IDS, SLOT))
+    upper = lax.broadcasted_iota(jnp.int32, (IDS, SLOT), 0) < IDS // 2
+    coded = jnp.where(upper, shifted >> 5, shifted & 31).astype(F32).astype(BF)
+    own_ids[...] = coded
+    kv[y, BLOCK:, :] = coded
 
     barrier = pltpu.get_barrier_semaphore()
-    for dy, dz, dc in others:
-        pl.semaphore_signal(barrier, inc=1, device_id=device(dy, dz, dc), device_id_type=MESH)
-    for d in range(1, n_pair):
-        pl.semaphore_signal(
-            barrier, inc=1, device_id=((pair + d) % n_pair, blk), device_id_type=MESH
-        )
-    pl.semaphore_wait(barrier, NBLK - 1 + n_pair - 1)
+    for step in column + plane:
+        pl.semaphore_signal(barrier, inc=1, device_id=across(*step), device_id_type=MESH)
+    pl.semaphore_wait(barrier, len(column) + len(plane))
 
     kv_copies = {}
     for dy in (1, 3, 2):
         to = device(dy, 0, 0)
-        for s, d in kv_parts((y + dy) % NY, y):
+        parts = kv_parts((y + dy) % NY, y) + ((own_ids, kv.at[y, pl.ds(BLOCK, IDS)]),)
+        for s, d in parts:
             remote(s, d, kv_send.at[dy], kv_recv.at[dy], to).start()
         kv_copies[dy] = remote(kv.at[y], kv.at[y], kv_send.at[dy], kv_recv.at[dy], to)
-    id_copies = []
-    for i, (dy, dz, dc) in enumerate(others):
-        copy = remote(
-            idb.at[y], idb.at[dz * 8 + dc * 4 + y], id_send.at[i], id_recv.at[i], device(dy, dz, dc)
-        )
-        copy.start()
-        id_copies.append(copy)
     q_copies = {}
     for dy in (2, 1, 3):
         q_copies[dy] = remote(
             q_hbm.at[:, columns((y + dy) % NY, WIDE)], qin.at[y],
             q_send.at[dy], q_recv.at[dy], device(dy, 0, 0),
         )
+    q_copies[2].start()
 
     z_copies, c_copies, zc_copies = {}, {}, {}
 
@@ -120,61 +126,47 @@
         copy.wait()
     forward(0)
 
-    for copy in id_copies:
-        copy.wait_recv()
-    rows = lax.broadcasted_iota(jnp.int32, (SLOT, SLOT), 0)
-    cols = lax.broadcasted_iota(jnp.int32, (SLOT, SLOT), 1)
-    same = rows == cols
-    turned = rows + cols == SLOT - 1
-    turn = jnp.where(turned, 1.0, 0.0).astype(BF)
-
-    def column_of(row, where):
-        return jnp.sum(jnp.where(where, row, 0.0), axis=1, keepdims=True)
-
-    def merged_ids(first, second):
-        col = column_of(idb[first][:1].astype(F32), same)
-        back = column_of(idb[second][:1].astype(F32), turned)
-        return col, jnp.where(col >= 0.0, col, back)
-
-    def key_ids(first, second):
-        live, ids = merged_ids(first, second)
-        return live, jnp.sum(jnp.where(same, ids, 0.0), axis=0, keepdims=True)
-
-    lives, id_rows = [], []
-    for g in range(4):
-        for j in range(2):
-            live, row = key_ids(4 * g + j, 4 * g + j + 2)
-            lives.append(live)
-            id_rows.append(row)
-    chosen_len = len_ref[:1, :1].astype(F32)
-    rejected_len = len_ref[:1, 1:2].astype(F32)
-    firsts = (y % 2, (y + 1) % 2)
-    for n in range(2):
-        _, ids = merged_ids(firsts[n], firsts[n] + 2)
-        lowest = jnp.where(ids >= chosen_len, chosen_len, 0.0)
-        qid[n] = jnp.broadcast_to(ids, (SLOT, HD))
-        for m in range(8):
-            visible = (id_rows[m] <= ids) & (id_rows[m] >= lowest)
-            bias[n, :, m * SLOT : (m + 1) * SLOT] = jnp.where(visible, HIGH, LOW)
-
     for dy in (1, 3):
         kv_copies[dy].wait_recv()
         forward(dy)
-    q_copies[2].start()
+    q_copies[1].start()
+    q_copies[3].start()
     kv_copies[2].wait_recv()
     forward(2)
-    q_copies[1].start()
-    q_copies[3].start()
+
+    rows = lax.broadcasted_iota(jnp.int32, (SLOT, SLOT), 0)
+    cols = lax.broadcasted_iota(jnp.int32, (SLOT, SLOT), 1)
+    eye = jnp.where(rows == cols, 1.0, 0.0).astype(BF)
+    turn = jnp.where(rows + cols == SLOT - 1, 1.0, 0.0).astype(BF)
+    half_ids = IDS // 2
+
+    def ids_in(slot):
+        return kv[slot, BLOCK:, :]
+
+    def column_ids(slot, order):
+        t = dot_t(order, ids_in(slot))
+        return 32.0 * t[:, :1] + t[:, half_ids : half_ids + 1] - 32.0
+
+    def row_ids(t):
+        return 32.0 * t[:1] + t[half_ids : half_ids + 1] - 32.0
+
+    def merged_column(first):
+        col = column_ids(first, eye)
+        return jnp.where(col >= 0.0, col, column_ids(first + 2, turn))
+
+    def merged_row(first):
+        row = row_ids(ids_in(first).astype(F32))
+        return jnp.where(row >= 0.0, row, row_ids(dot(ids_in(first + 2), turn)))
+
+    firsts = (y % 2, (y + 1) % 2)
 
     def load_queries(n):
         first = firsts[n]
-        live = qid[n]
-        col = column_of(idb[first][:1].astype(F32), same)
+        live = column_ids(first, eye) >= 0.0
         back = dot(turn, qin[first + 2])
-        del live
         for h in range(GROUP):
             at = slice(h * HD, (h + 1) * HD)
-            x = jnp.where(col >= 0.0, qin[first, :, at].astype(F32), back[:, at]) * SCALE
+            x = jnp.where(live, qin[first, :, at].astype(F32), back[:, at]) * SCALE
             high = x.astype(BF)
             qs[n, at, :HD] = high
             qs[n, at, HD:] = (x - high.astype(F32)).astype(BF)
@@ -245,11 +237,22 @@
     for dy in range(NY):
         zc_copies[dy].wait_recv()
 
+    id_rows = [merged_row(4 * g + j) for g in range(4) for j in range(2)]
+    chosen_len = len_ref[:1, :1].astype(F32)
+    rejected_len = len_ref[:1, 1:2].astype(F32)
+    for n in range(2):
+        ids = merged_column(firsts[n])
+        lowest = jnp.where(ids >= chosen_len, chosen_len, 0.0)
+        qid[n] = jnp.broadcast_to(ids, (SLOT, HD))
+        for m in range(8):
+            visible = (id_rows[m] <= ids) & (id_rows[m] >= lowest)
+            bias[n, :, m * SLOT : (m + 1) * SLOT] = jnp.where(visible, HIGH, LOW)
+
     for g in range(4):
         for j in range(2):
             m = 2 * g + j
-            live = lives[m] >= 0.0
-            tail = slice(2 * PKEYS, 2 * PKEYS + 2 * SLOT)
+            live = column_ids(4 * g + j, eye) >= 0.0
+            tail = slice(2 * PKEYS, BLOCK)
             one = kv[4 * g + j, tail, :].astype(F32)
             two = kv[4 * g + j + 2, tail, :]
             at = slice(m * SLOT, (m + 1) * SLOT)
@@ -311,34 +314,34 @@
         first = qid[n] < chosen_len
         chosen = chosen + total_of(jnp.where(first, score[n], 0.0))
         rejected = rejected + total_of(jnp.where(first, 0.0, score[n]))
-    lane = lax.broadcasted_iota(jnp.int32, (8, HD), 1)
-    part[blk] = jnp.where(lane == 0, chosen, jnp.where(lane == 1, rejected, 0.0))
+    lane = lax.broadcasted_iota(jnp.int32, (PAIRS, HD), 1)
+    mine = lax.broadcasted_iota(jnp.int32, (PAIRS, HD), 0) == pair
+    tile = jnp.where(lane == 0, chosen / chosen_len, rejected / rejected_len)
+    z_place = z4 * 2 + c
+    part[z_place] = jnp.where(mine & (lane < 2), tile, 0.0)
     p_copies = []
-    for i, (dy, dz, dc) in enumerate(others):
+    for i, step in enumerate(column):
         copy = remote(
-            part.at[blk], part.at[blk], p_send.at[i], p_recv.at[i], device(dy, dz, dc)
+            part.at[z_place], part.at[z_place], p_send.at[i], p_recv.at[i], across(*step)
         )
         copy.start()
         p_copies.append(copy)
     for copy in p_copies:
         copy.wait_recv()
     sums = part[0]
-    for i in range(1, NBLK):
+    for i in range(1, 8):
         sums = sums + part[i]
-    margin = sums[:1, :1] / chosen_len - sums[:1, 1:2] / rejected_len
-    x = -4.0 * margin
-    value = jnp.maximum(x, 0.0) + jnp.log1p(jnp.exp(-jnp.abs(x)))
-    term[pair] = jnp.broadcast_to(value, (8, HD))
+    place_xy = x * NY + y
+    whole_sums[place_xy] = sums
     t_copies = []
-    for d in range(1, n_pair):
+    for i, step in enumerate(plane):
         copy = remote(
-            term.at[pair], term.at[pair], t_send.at[d - 1], t_recv.at[d - 1],
-            ((pair + d) % n_pair, blk),
+            whole_sums.at[place_xy], whole_sums.at[place_xy], t_send.at[i], t_recv.at[i], across(*step)
         )
         copy.start()
         t_copies.append(copy)
 
-    live = column_of(idb[y][:1].astype(F32), same) >= 0.0
+    live = column_ids(y, eye) >= 0.0
     back = y >= 2
     take = jnp.where(back, SLOT - 1 - rows, rows) == cols
     place = jnp.where(live & take, 1.0, 0.0).astype(BF)
@@ -358,10 +361,12 @@
 
     for copy in t_copies:
         copy.wait_recv()
-    loss = term[0]
-    for i in range(1, n_pair):
-        loss = loss + term[i]
-    loss_ref[...] = loss[:1, :1]
+    sums = whole_sums[0]
+    for i in range(1, 16):
+        sums = sums + whole_sums[i]
+    value = -4.0 * (sums[:, :1] - sums[:, 1:2])
+    terms = jnp.maximum(value, 0.0) + jnp.log1p(jnp.exp(-jnp.abs(value)))
+    loss_ref[...] = jnp.sum(terms, axis=0, keepdims=True)
 
     for dy in (1, 2, 3):
         kv_copies[dy].wait_send()
@@ -374,16 +379,16 @@
         for i in range(2):
             for copy in out_copies(n, i):
                 copy.wait_send()
-    for copy in id_copies + p_copies + t_copies:
+    for copy in p_copies + t_copies:
         copy.wait_send()
 
 
-def local(n_pair, queries, prompt_keys, prompt_values, resp_keys, resp_values, slot_row, lengths, probe):
+def local(queries, prompt_keys, prompt_values, resp_keys, resp_values, slot_row, lengths, probe):
     vmem = pl.BlockSpec(memory_space=pltpu.VMEM)
     anywhere = pl.BlockSpec(memory_space=pl.ANY)
     sems = pltpu.SemaphoreType.DMA
     attended, loss = pl.pallas_call(
-        functools.partial(kernel, n_pair),
+        kernel,
         out_shape=(
             jax.ShapeDtypeStruct((SLOT, QH * HD), BF),
             jax.ShapeDtypeStruct((1, 1), F32),
@@ -391,8 +396,8 @@
         in_specs=[anywhere] * 5 + [vmem] * 3,
         out_specs=(vmem, vmem),
         scratch_shapes=[
-            pltpu.VMEM((NBLK, 2 * PKEYS + 2 * SLOT, HD), BF),
-            pltpu.VMEM((NBLK, 8, SLOT), jnp.int32),
+            pltpu.VMEM((NBLK, BLOCK + IDS, HD), BF),
+            pltpu.VMEM((IDS, SLOT), BF),
             pltpu.VMEM((NY, SLOT, WIDE), BF),
             pltpu.VMEM((2, WIDE, 2 * HD), BF),
             pltpu.VMEM((8 * SLOT, HD), BF),
@@ -404,18 +409,17 @@
             pltpu.VMEM((2, SLOT, HD), F32),
             pltpu.VMEM((2, 2, SLOT, WIDE // 2), BF),
             pltpu.VMEM((NY, 2, SLOT, WIDE // 2), BF),
-            pltpu.VMEM((NBLK, 8, HD), F32),
-            pltpu.VMEM((n_pair, 8, HD), F32),
+            pltpu.VMEM((8, PAIRS, HD), F32),
+            pltpu.VMEM((16, PAIRS, HD), F32),
             sems((5,)),
             sems((NY,)), sems((NY,)),
             sems((NY,)), sems((NY,)),
             sems((NY,)), sems((NY,)),
             sems((NY,)), sems((NY,)),
-            sems((NBLK - 1,)), sems((NBLK - 1,)),
             sems((NY,)), sems((NY,)),
             sems((NY, 2)), sems((NY, 2)),
-            sems((NBLK - 1,)), sems((NBLK - 1,)),
-            sems((8,)), sems((8,)),
+            sems((7,)), sems((7,)),
+            sems((15,)), sems((15,)),
         ],
         compiler_params=pltpu.CompilerParams(
             collective_id=0, has_side_effects=True, vmem_limit_bytes=56 * 2**20
@@ -432,7 +436,7 @@
 
 def solution(mesh):
     return jax.shard_map(
-        functools.partial(local, mesh.shape["pair"]),
+        local,
         mesh=mesh,
         in_specs=(
             P("pair", "blk", None),

time: 68.5 us -> 61.5 us (0.90)
  Pallas kernels: 63.5 us -> 56.5 us
    pallas_call x1, Pallas kernels: 63.5 us -> 56.5 us  [local(): pl.pallas_call(kernel, out_shape=(jax.ShapeDtypeStruct((SLOT, QH * HD), B...]
where the time goes in v2:
time: 61.5 us; the launch traced here: 61.1 us
  Pallas kernels  56.5 us (92%)
  between operations  2.33 us (4%)
  local copies, waits for them, and re-layouts  2.29 us (4%)
    pallas_call x1, Pallas kernels, local(): pl.pallas_call(kernel, out_shape=(jax.ShapeDtypeStruct((SLOT, QH * HD), B...  56.5 us
    unnamed x1, local copies, waits for them, and re-layouts  2.29 us

profile of v2, /device:TPU:1, one launch (start us, length us, event | category | flops | bytes accessed | tf_op | source)
XLA Modules:
  0.0 61.1 jit_solution(8560339387594830576)
XLA Ops:
  0.6 56.5 %shard_map.95 = (bf16[128,4096]{1,0:T(8,128)(2,1)}, f32[1,1]{1,0:T(1,128)}) custom-call(bf16[128,4096]{1,0:T(8,128)(2,1)} %bitcast.9, bf16[256,512]{1,0:T(8,128)(2,1)} %bitcast.10, bf16[256,512]{1,0:T(8,128)(2,1)} %bitcast.11, bf16[128,512]{1,0:T(8,128)(2,1)} %bitcast.12, bf16[128,512]{1,0:T(8,128)(2,1)} %bitcast.13, s32[1,128]{1,0:T(1,128)} %slot_ref.1, ...), custom_call_target="tpu_custom_call" | custom-call | flops 5400000000 | bytes 4000000 | tf_op jit(solution)/shard_map/pallas_call | solution.py:390
  57.1 2.3 %copy.12 = bf16[1,128,4096]{2,1,0:T(8,128)(2,1)} copy(bf16[1,128,4096]{2,1,0:T(8,128)(2,1)} %bitcast.8) | data formatting | bytes 2097152

commit v3 on v2

v3 whole, which is shorter than its diff:
```python
import functools

import jax
import jax.numpy as jnp
from jax import lax
from jax.experimental import pallas as pl
from jax.experimental.pallas import tpu as pltpu
from jax.sharding import PartitionSpec as P

QH = 32
KVH = 4
HD = 128
GROUP = QH // KVH
SLOT = 128
PKEYS = 256
NY = 4
NBLK = 16
PAIRS = 8
IDS = 16
RESP = 2 * SLOT
WIDE = GROUP * HD
SCALE = 1.4426950408889634 / HD**0.5
MESH = pl.DeviceIdType.MESH
BF = jnp.bfloat16
F32 = jnp.float32
LOW = -1e30
HIGH = 3e38


def dot_t(a, b):
    return lax.dot_general(a, b, (((1,), (1,)), ((), ())), preferred_element_type=F32)


def dot(a, b):
    return jnp.dot(a, b, preferred_element_type=F32)


def kernel(
    q_hbm, kp_hbm, vp_hbm, kr_hbm, vr_hbm, slot_hbm, len_hbm, probe_hbm,
    att_hbm, loss_ref,
    slot_ref, len_ref, probe_ref, att, kv, resp, merged, ids, qin, qs, bias, qid, top, acc, score, osend, oin, part, whole_sums,
    local_sem, small_sem, att_sem, kv_send, kv_recv, r_send, r_recv, id_send, id_recv, z_send, z_recv, c_send, c_recv, zc_send, zc_recv,
    q_send, q_recv, o_send, o_recv, p_send, p_recv, t_send, t_recv,
):
    pair = lax.axis_index("pair")
    blk = lax.axis_index("blk")
    y, z, c = blk // 4, (blk // 2) % 2, blk % 2
    x, z4 = pair % 4, pair // 4 * 2 + z

    def device(dy, dz, dc):
        return (pair, ((y + dy) % NY) * 4 + ((z + dz) % 2) * 2 + (c + dc) % 2)

    def across(dx, dy, dz4, dc):
        to = (z4 + dz4) % 4
        return (
            to // 2 * 4 + (x + dx) % 4,
            ((y + dy) % NY) * 4 + (to % 2) * 2 + (c + dc) % 2,
        )

    column = [(0, 0, dz4, dc) for dz4 in range(4) for dc in range(2)][1:]
    plane = [(dx, dy, 0, 0) for dx in range(4) for dy in range(NY)][1:]

    def remote(src, dst, send, recv, target):
        return pltpu.make_async_remote_copy(
            src_ref=src, dst_ref=dst, send_sem=send, recv_sem=recv,
            device_id=target, device_id_type=MESH,
        )

    def columns(head, width):
        return pl.ds(pl.multiple_of(head * width, width), width)

    def prompt_parts(head):
        cols = columns(head, HD)
        return (
            (kp_hbm.at[:, cols], kv.at[0, y, pl.ds(0, PKEYS)]),
            (vp_hbm.at[:, cols], kv.at[0, y, pl.ds(PKEYS, PKEYS)]),
        )

    def resp_parts(head):
        cols = columns(head, HD)
        return (
            (kr_hbm.at[:, cols], resp.at[y, pl.ds(0, SLOT)]),
            (vr_hbm.at[:, cols], resp.at[y, pl.ds(SLOT, SLOT)]),
        )

    own = [
        pltpu.make_async_copy(s, d, local_sem.at[i])
        for i, (s, d) in enumerate(prompt_parts(y) + resp_parts(y))
    ]
    own_q = [
        pltpu.make_async_copy(
            q_hbm.at[:, columns(y * 2 + i, WIDE // 2)], qin.at[y, i], local_sem.at[4 + i]
        )
        for i in range(2)
    ]
    for copy in own + own_q:
        copy.start()
    small = [
        pltpu.make_async_copy(s, d, small_sem.at[i])
        for i, (s, d) in enumerate(
            ((slot_hbm, slot_ref), (len_hbm, len_ref), (probe_hbm, probe_ref))
        )
    ]
    for copy in small:
        copy.start()

    small[0].wait()
    shifted = jnp.broadcast_to(slot_ref[...] + 32, (IDS, SLOT))
    upper = lax.broadcasted_iota(jnp.int32, (IDS, SLOT), 0) < IDS // 2
    ids[y] = jnp.where(upper, shifted >> 5, shifted & 31).astype(F32).astype(BF)

    barrier = pltpu.get_barrier_semaphore()
    for step in column + plane:
        pl.semaphore_signal(barrier, inc=1, device_id=across(*step), device_id_type=MESH)
    pl.semaphore_wait(barrier, len(column) + len(plane))

    kv_copies, r_copies, q_copies = {}, {}, {}

    def send_prompt(dy):
        to = device(dy, 0, 0)
        for s, d in prompt_parts((y + dy) % NY):
            remote(s, d, kv_send.at[dy], kv_recv.at[dy], to).start()
        kv_copies[dy] = remote(kv.at[0, y], kv.at[0, y], kv_send.at[dy], kv_recv.at[dy], to)

    def send_resp(dy):
        to = device(dy, 0, 0)
        for s, d in resp_parts((y + dy) % NY):
            remote(s, d, r_send.at[dy], r_recv.at[dy], to).start()
        r_copies[dy] = remote(resp.at[y], resp.at[y], r_send.at[dy], r_recv.at[dy], to)

    for dy in (1, 2, 3):
        for i in range(2):
            q_copies[dy, i] = remote(
                q_hbm.at[:, columns(((y + dy) % NY) * 2 + i, WIDE // 2)], qin.at[y, i],
                q_send.at[dy, i], q_recv.at[dy, i], device(dy, 0, 0),
            )

    def send_queries(dy, i):
        q_copies[dy, i].start()

    id_copies = {
        dy: remote(ids.at[y], ids.at[y], id_send.at[dy], id_recv.at[dy], device(dy, 0, 0))
        for dy in (1, 2, 3)
    }
    send_prompt(1)
    send_prompt(3)
    for dy in (1, 2, 3):
        id_copies[dy].start()

    z_copies, c_copies, zc_copies = {}, {}, {}

    def pass_on(name, piece):
        z_copies[name] = remote(
            piece(0), piece(2), z_send.at[name], z_recv.at[name], device(0, 1, 0)
        )
        c_copies[name] = remote(
            piece(0), piece(1), c_send.at[name], c_recv.at[name], device(0, 0, 1)
        )
        zc_copies[name] = remote(
            piece(2), piece(3), zc_send.at[name], zc_recv.at[name], device(0, 0, 1)
        )

    def start_on(name):
        z_copies[name].start()
        c_copies[name].start()

    def forward(dy):
        at = (y - dy + NY) % NY
        pass_on(dy, lambda group: kv.at[group, at])
        start_on(dy)

    for copy in own:
        copy.wait()
    forward(0)

    c_copies[0].wait_recv()
    send_prompt(2)
    for dy in (1, 3):
        kv_copies[dy].wait_recv()
        forward(dy)
    send_queries(2, 0)
    kv_copies[2].wait_recv()
    forward(2)
    for dy in (1, 3, 2):
        send_resp(dy)

    rows = lax.broadcasted_iota(jnp.int32, (SLOT, SLOT), 0)
    cols = lax.broadcasted_iota(jnp.int32, (SLOT, SLOT), 1)
    eye = jnp.where(rows == cols, 1.0, 0.0).astype(BF)
    turn = jnp.where(rows + cols == SLOT - 1, 1.0, 0.0).astype(BF)
    half_ids = IDS // 2

    def column_ids(slot, order):
        t = dot_t(order, ids[slot])
        return 32.0 * t[:, :1] + t[:, half_ids : half_ids + 1] - 32.0

    def row_ids(t):
        return 32.0 * t[:1] + t[half_ids : half_ids + 1] - 32.0

    firsts = (y % 2, (y + 1) % 2)

    def load_queries(n, i):
        first = firsts[n]
        live = column_ids(first, eye) >= 0.0
        back = dot(turn, qin[first + 2, i])
        for h in range(GROUP // 2):
            at = slice(h * HD, (h + 1) * HD)
            to = slice((i * (GROUP // 2) + h) * HD, (i * (GROUP // 2) + h + 1) * HD)
            x = jnp.where(live, qin[first, i, :, at].astype(F32), back[:, at]) * SCALE
            high = x.astype(BF)
            qs[n, to, :HD] = high
            qs[n, to, HD:] = (x - high.astype(F32)).astype(BF)

    def twice(k):
        return jnp.concatenate([k, k], axis=1)

    def with_ones(v):
        return jnp.concatenate([v, jnp.ones_like(v)], axis=1)

    def prompt(groups, at):
        part = kv[groups, :, at : at + PKEYS, :]
        return part.reshape(part.shape[0] * NY * PKEYS, HD)

    def response(at):
        return merged[:, :, at : at + SLOT, :].reshape(8 * SLOT, HD)

    HALF = 2 * HD

    def scores(n, i, keys):
        q = [qs[n, pl.ds(i * 2 * HALF + j * HALF, HALF), :] for j in range(2)]
        return [dot_t(x, keys) for x in q]

    def masked(n, s):
        at = s.shape[1] - 8 * SLOT
        limit = bias[n]
        limit = jnp.concatenate([limit, limit], axis=0)
        return jnp.concatenate([s[:, :at], jnp.minimum(s[:, at:], limit)], axis=1)

    def highest(s):
        return jnp.max(s, axis=1, keepdims=True)

    def weigh(s, high, values):
        return dot(jnp.exp2(s - high).astype(BF), values)

    def finish(n, i, j, result):
        out = (result[:, :HD] / result[:, HD:]).astype(BF)
        for h in range(2):
            head = 2 * j + h
            x = out[h * HD : (h + 1) * HD]
            osend[n, i, :, head * HD : (head + 1) * HD] = x
            weights = probe_ref[pl.ds(y * GROUP + i * 4 + head, 1), :]
            score[n] = score[n] + x.astype(F32) * weights

    score[...] = jnp.zeros_like(score)

    def take_z(name):
        z_copies[name].wait_recv()
        zc_copies[name].start()

    pass_on(NY, lambda group: merged.at[group])

    def merge():
        for dy in (1, 3, 2):
            r_copies[dy].wait_recv()
        for j in range(2):
            live = column_ids(j, eye) >= 0.0
            for part_of in range(2):
                at = slice(part_of * SLOT, (part_of + 1) * SLOT)
                one = resp[j, at, :].astype(F32)
                two = dot(turn, resp[j + 2, at, :])
                merged[0, j, at, :] = jnp.where(live, one, two).astype(BF)
            one = ids[j].astype(F32)
            two = dot(ids[j + 2], turn)
            merged[0, j, RESP:, :] = jnp.where(row_ids(one) >= 0.0, one, two).astype(BF)
        start_on(NY)

    def near(k, carry):
        @pl.when(k == 0)
        def _():
            own_q[0].wait()
            q_copies[2, 0].wait_recv()
            send_queries(2, 1)
            for dy in (1, 2, 3):
                id_copies[dy].wait_recv()
            load_queries(0, 0)
            for dy in (1, 2, 3):
                c_copies[dy].wait_recv()

        @pl.when(k == 1)
        def _():
            merge()
            send_queries(1, 0)
            send_queries(3, 0)
            for name in (0, 1, 3):
                take_z(name)
            own_q[1].wait()
            q_copies[2, 1].wait_recv()
            send_queries(1, 1)
            send_queries(3, 1)
            load_queries(0, 1)

        plane = slice(0, 2)
        keys, values = twice(prompt(plane, 0)), with_ones(prompt(plane, PKEYS))
        for j, s in enumerate(scores(0, k, keys)):
            high = highest(s)
            at = pl.ds(k * 2 * HALF + j * HALF, HALF)
            top[at, :] = jnp.broadcast_to(high, (HALF, HD))
            acc[at, :] = weigh(s, high, values)
        return carry

    lax.fori_loop(0, 2, near, 0)

    for name in (2, NY):
        take_z(name)
    c_copies[NY].wait_recv()
    for name in range(NY + 1):
        zc_copies[name].wait_recv()

    id_rows = [
        row_ids(merged[g, j, RESP:, :].astype(F32)) for g in range(4) for j in range(2)
    ]
    small[1].wait()
    small[2].wait()
    chosen_len = len_ref[:1, :1].astype(F32)
    rejected_len = len_ref[:1, 1:2].astype(F32)
    for n in range(2):
        t = dot_t(eye, merged[0, firsts[n], RESP:, :])
        row_of = 32.0 * t[:, :1] + t[:, half_ids : half_ids + 1] - 32.0
        lowest = jnp.where(row_of >= chosen_len, chosen_len, 0.0)
        qid[n] = jnp.broadcast_to(row_of, (SLOT, HD))
        for m in range(8):
            visible = (id_rows[m] <= row_of) & (id_rows[m] >= lowest)
            bias[n, :, m * SLOT : (m + 1) * SLOT] = jnp.where(visible, HIGH, LOW)

    def out_copies(n, i):
        return [
            remote(
                osend.at[n, i], oin.at[y, i],
                o_send.at[dy, i], o_recv.at[dy, i], device(dy, 0, 0),
            )
            for dy in ((2,), (1, 3))[n]
        ]

    def far(i, carry):
        plane = slice(2, 4)
        keys = twice(jnp.concatenate([prompt(plane, 0), response(0)], axis=0))
        values = with_ones(jnp.concatenate([prompt(plane, PKEYS), response(SLOT)], axis=0))
        for j, s in enumerate(scores(0, i, keys)):
            s = masked(0, s)
            at = pl.ds(i * 2 * HALF + j * HALF, HALF)
            before = top[at, :]
            high = jnp.maximum(before, highest(s))
            factor = jnp.exp2(before - high)
            result = weigh(s, high[:, :1], values)
            total = acc[at, :] * jnp.concatenate([factor, factor], axis=1) + result
            finish(0, i, j, total)
        for copy in out_copies(0, i):
            copy.start()
        return carry

    lax.fori_loop(0, 2, far, 0)

    def whole(i, carry):
        for half in range(2):

            @pl.when(i == half)
            def _():
                q_copies[1, half].wait_recv()
                q_copies[3, half].wait_recv()
                load_queries(1, half)

        both = slice(0, 4)
        keys = twice(jnp.concatenate([prompt(both, 0), response(0)], axis=0))
        values = with_ones(jnp.concatenate([prompt(both, PKEYS), response(SLOT)], axis=0))
        for j, s in enumerate(scores(1, i, keys)):
            s = masked(1, s)
            finish(1, i, j, weigh(s, highest(s), values))
        for copy in out_copies(1, i):
            copy.start()
        return carry

    lax.fori_loop(0, 2, whole, 0)

    chosen = jnp.zeros((1, 1), F32)
    rejected = jnp.zeros((1, 1), F32)

    def total_of(x):
        return jnp.sum(jnp.sum(x, axis=1, keepdims=True), axis=0, keepdims=True)

    for n in range(2):
        first = qid[n] < chosen_len
        chosen = chosen + total_of(jnp.where(first, score[n], 0.0))
        rejected = rejected + total_of(jnp.where(first, 0.0, score[n]))
    lane = lax.broadcasted_iota(jnp.int32, (PAIRS, HD), 1)
    mine = lax.broadcasted_iota(jnp.int32, (PAIRS, HD), 0) == pair
    tile = jnp.where(lane == 0, chosen / chosen_len, rejected / rejected_len)
    z_place = z4 * 2 + c
    part[z_place] = jnp.where(mine & (lane < 2), tile, 0.0)
    p_copies = []
    for i, step in enumerate(column):
        copy = remote(
            part.at[z_place], part.at[z_place], p_send.at[i], p_recv.at[i], across(*step)
        )
        copy.start()
        p_copies.append(copy)
    for copy in p_copies:
        copy.wait_recv()
    sums = part[0]
    for i in range(1, 8):
        sums = sums + part[i]
    place_xy = x * NY + y
    whole_sums[place_xy] = sums
    t_copies = []
    for i, step in enumerate(plane):
        copy = remote(
            whole_sums.at[place_xy], whole_sums.at[place_xy], t_send.at[i], t_recv.at[i], across(*step)
        )
        copy.start()
        t_copies.append(copy)

    live = column_ids(y, eye) >= 0.0
    back = y >= 2
    take = jnp.where(back, SLOT - 1 - rows, rows) == cols
    place = jnp.where(live & take, 1.0, 0.0).astype(BF)

    att_copies = []

    def put(head, i, x):
        at = columns(head * 2 + i, WIDE // 2)
        k = len(att_copies)
        att[k] = dot(place, x).astype(BF)
        copy = pltpu.make_async_copy(att.at[k], att_hbm.at[:, at], att_sem.at[k])
        copy.start()
        att_copies.append(copy)

    for i in range(2):
        put(y, i, osend[0, i])
    for n, dys in enumerate(((2,), (1, 3))):
        for i in range(2):
            for copy, dy in zip(out_copies(n, i), dys):
                copy.wait_recv()
                source = (y - dy + NY) % NY
                put(source, i, oin[source, i])

    for copy in t_copies:
        copy.wait_recv()
    sums = whole_sums[0]
    for i in range(1, 16):
        sums = sums + whole_sums[i]
    value = -4.0 * (sums[:, :1] - sums[:, 1:2])
    terms = jnp.maximum(value, 0.0) + jnp.log1p(jnp.exp(-jnp.abs(value)))
    loss_ref[...] = jnp.sum(terms, axis=0, keepdims=True)

    for copy in att_copies:
        copy.wait()
    for dy in (1, 2, 3):
        kv_copies[dy].wait_send()
        r_copies[dy].wait_send()
        id_copies[dy].wait_send()
        for i in range(2):
            q_copies[dy, i].wait_send()
    for name in range(NY + 1):
        z_copies[name].wait_send()
        c_copies[name].wait_send()
        zc_copies[name].wait_send()
    for n in range(2):
        for i in range(2):
            for copy in out_copies(n, i):
                copy.wait_send()
    for copy in p_copies + t_copies:
        copy.wait_send()


def local(queries, prompt_keys, prompt_values, resp_keys, resp_values, slot_row, lengths, probe):
    vmem = pl.BlockSpec(memory_space=pltpu.VMEM)
    anywhere = pl.BlockSpec(memory_space=pl.ANY)
    sems = pltpu.SemaphoreType.DMA
    attended, loss = pl.pallas_call(
        kernel,
        out_shape=(
            jax.ShapeDtypeStruct((SLOT, QH * HD), BF),
            jax.ShapeDtypeStruct((1, 1), F32),
        ),
        in_specs=[anywhere] * 8,
        out_specs=(anywhere, vmem),
        scratch_shapes=[
            pltpu.VMEM((1, SLOT), jnp.int32),
            pltpu.VMEM((1, 2), jnp.int32),
            pltpu.VMEM((QH, HD), F32),
            pltpu.VMEM((2 * NY, SLOT, WIDE // 2), BF),
            pltpu.VMEM((4, NY, 2 * PKEYS, HD), BF),
            pltpu.VMEM((NY, RESP, HD), BF),
            pltpu.VMEM((4, 2, RESP + IDS, HD), BF),
            pltpu.VMEM((NY, IDS, SLOT), BF),
            pltpu.VMEM((NY, 2, SLOT, WIDE // 2), BF),
            pltpu.VMEM((2, WIDE, 2 * HD), BF),
            pltpu.VMEM((2, SLOT, 8 * SLOT), F32),
            pltpu.VMEM((2, SLOT, HD), F32),
            pltpu.VMEM((WIDE, HD), F32),
            pltpu.VMEM((WIDE, 2 * HD), F32),
            pltpu.VMEM((2, SLOT, HD), F32),
            pltpu.VMEM((2, 2, SLOT, WIDE // 2), BF),
            pltpu.VMEM((NY, 2, SLOT, WIDE // 2), BF),
            pltpu.VMEM((8, PAIRS, HD), F32),
            pltpu.VMEM((16, PAIRS, HD), F32),
            sems((6,)),
            sems((3,)),
            sems((2 * NY,)),
            sems((NY,)), sems((NY,)),
            sems((NY,)), sems((NY,)),
            sems((NY,)), sems((NY,)),
            sems((NY + 1,)), sems((NY + 1,)),
            sems((NY + 1,)), sems((NY + 1,)),
            sems((NY + 1,)), sems((NY + 1,)),
            sems((NY, 2)), sems((NY, 2)),
            sems((NY, 2)), sems((NY, 2)),
            sems((7,)), sems((7,)),
            sems((15,)), sems((15,)),
        ],
        compiler_params=pltpu.CompilerParams(
            collective_id=0, has_side_effects=True, vmem_limit_bytes=56 * 2**20
        ),
        cost_estimate=pl.CostEstimate(
            flops=5_400_000_000, bytes_accessed=4_000_000, transcendentals=10_500_000
        ),
    )(
        queries[0], prompt_keys[0], prompt_values[0], resp_keys[0], resp_values[0],
        slot_row, lengths, probe.reshape(QH, HD),
    )
    return attended[None], loss[0, 0]


def solution(mesh):
    return jax.shard_map(
        local,
        mesh=mesh,
        in_specs=(
            P("pair", "blk", None),
            P("pair", "blk", None),
            P("pair", "blk", None),
            P("pair", "blk", None),
            P("pair", "blk", None),
            P("pair", "blk"),
            P("pair", None),
            P(),
        ),
        out_specs=(P("pair", "blk", None), P()),
        check_vma=False,
    )
```

time: 61.5 us -> 56.4 us (0.917)
  Pallas kernels: 56.5 us -> 51.6 us
    pallas_call x1, Pallas kernels: 56.5 us -> 51.6 us  [local(): pl.pallas_call(kernel, out_shape=(jax.ShapeDtypeStruct((SLOT, QH * HD), B...]
where the time goes in v3:
time: 56.4 us; the launch traced here: 56.3 us
  Pallas kernels  51.6 us (91%)
  between operations  2.33 us (4%)
  local copies, waits for them, and re-layouts  2.29 us (4%)
    pallas_call x1, Pallas kernels, local(): pl.pallas_call(kernel, out_shape=(jax.ShapeDtypeStruct((SLOT, QH * HD), B...  51.6 us
    unnamed x1, local copies, waits for them, and re-layouts  2.29 us

profile of v3, /device:TPU:1, one launch (start us, length us, event | category | flops | bytes accessed | tf_op | source)
XLA Modules:
  0.0 56.3 jit_solution(1298564920771691998)
XLA Ops:
  0.6 51.6 %shard_map.95 = (bf16[128,4096]{1,0:T(8,128)(2,1)}, f32[1,1]{1,0:T(1,128)}) custom-call(bf16[128,4096]{1,0:T(8,128)(2,1)} %bitcast.9, bf16[256,512]{1,0:T(8,128)(2,1)} %bitcast.10, bf16[256,512]{1,0:T(8,128)(2,1)} %bitcast.11, bf16[128,512]{1,0:T(8,128)(2,1)} %bitcast.12, bf16[128,512]{1,0:T(8,128)(2,1)} %bitcast.13, s32[1,128]{1,0:T(1,128)} %slot_hbm.1, ...), custom_call_target="tpu_custom_call" | custom-call | flops 5400000000 | bytes 4000000 | tf_op jit(solution)/shard_map/pallas_call | solution.py:478
  52.3 2.3 %copy.12 = bf16[1,128,4096]{2,1,0:T(8,128)(2,1)} copy(bf16[1,128,4096]{2,1,0:T(8,128)(2,1)} %bitcast.8) | data formatting | bytes 2097152

commit v4 on v3

--- a/solution.py
+++ b/solution.py
@@ -104,14 +104,13 @@
     for copy in small:
         copy.start()
 
+    barrier = pltpu.get_barrier_semaphore()
+    for step in column + plane:
+        pl.semaphore_signal(barrier, inc=1, device_id=across(*step), device_id_type=MESH)
     small[0].wait()
     shifted = jnp.broadcast_to(slot_ref[...] + 32, (IDS, SLOT))
     upper = lax.broadcasted_iota(jnp.int32, (IDS, SLOT), 0) < IDS // 2
     ids[y] = jnp.where(upper, shifted >> 5, shifted & 31).astype(F32).astype(BF)
-
-    barrier = pltpu.get_barrier_semaphore()
-    for step in column + plane:
-        pl.semaphore_signal(barrier, inc=1, device_id=across(*step), device_id_type=MESH)
     pl.semaphore_wait(barrier, len(column) + len(plane))
 
     kv_copies, r_copies, q_copies = {}, {}, {}
@@ -178,11 +177,12 @@
     for dy in (1, 3):
         kv_copies[dy].wait_recv()
         forward(dy)
-    send_queries(2, 0)
+    for dy in (2, 1, 3):
+        send_resp(dy)
     kv_copies[2].wait_recv()
     forward(2)
-    for dy in (1, 3, 2):
-        send_resp(dy)
+    c_copies[2].wait_recv()
+    send_queries(2, 0)
 
     rows = lax.broadcasted_iota(jnp.int32, (SLOT, SLOT), 0)
     cols = lax.broadcasted_iota(jnp.int32, (SLOT, SLOT), 1)
@@ -196,6 +196,25 @@
 
     def row_ids(t):
         return 32.0 * t[:1] + t[half_ids : half_ids + 1] - 32.0
+
+    pass_on(NY, lambda group: merged.at[group])
+
+    for dy in (1, 2, 3):
+        id_copies[dy].wait_recv()
+    for dy in (1, 3, 2):
+        r_copies[dy].wait_recv()
+    for j in range(2):
+        live = column_ids(j, eye) >= 0.0
+        for part_of in range(2):
+            at = slice(part_of * SLOT, (part_of + 1) * SLOT)
+            one = resp[j, at, :].astype(F32)
+            two = dot(turn, resp[j + 2, at, :])
+            merged[0, j, at, :] = jnp.where(live, one, two).astype(BF)
+        one = ids[j].astype(F32)
+        two = dot(ids[j + 2], turn)
+        merged[0, j, RESP:, :] = jnp.where(row_ids(one) >= 0.0, one, two).astype(BF)
+    start_on(NY)
+    send_queries(2, 1)
 
     firsts = (y % 2, (y + 1) % 2)
 
@@ -257,41 +276,20 @@
         z_copies[name].wait_recv()
         zc_copies[name].start()
 
-    pass_on(NY, lambda group: merged.at[group])
-
-    def merge():
-        for dy in (1, 3, 2):
-            r_copies[dy].wait_recv()
-        for j in range(2):
-            live = column_ids(j, eye) >= 0.0
-            for part_of in range(2):
-                at = slice(part_of * SLOT, (part_of + 1) * SLOT)
-                one = resp[j, at, :].astype(F32)
-                two = dot(turn, resp[j + 2, at, :])
-                merged[0, j, at, :] = jnp.where(live, one, two).astype(BF)
-            one = ids[j].astype(F32)
-            two = dot(ids[j + 2], turn)
-            merged[0, j, RESP:, :] = jnp.where(row_ids(one) >= 0.0, one, two).astype(BF)
-        start_on(NY)
-
     def near(k, carry):
         @pl.when(k == 0)
         def _():
             own_q[0].wait()
             q_copies[2, 0].wait_recv()
-            send_queries(2, 1)
-            for dy in (1, 2, 3):
-                id_copies[dy].wait_recv()
+            send_queries(1, 0)
+            send_queries(3, 0)
             load_queries(0, 0)
-            for dy in (1, 2, 3):
+            for dy in (1, 3):
                 c_copies[dy].wait_recv()
 
         @pl.when(k == 1)
         def _():
-            merge()
-            send_queries(1, 0)
-            send_queries(3, 0)
-            for name in (0, 1, 3):
+            for name in (0, 1, 3, 2, NY):
                 take_z(name)
             own_q[1].wait()
             q_copies[2, 1].wait_recv()
@@ -310,8 +308,6 @@
 
     lax.fori_loop(0, 2, near, 0)
 
-    for name in (2, NY):
-        take_z(name)
     c_copies[NY].wait_recv()
     for name in range(NY + 1):
         zc_copies[name].wait_recv()

time: 56.4 us -> 54.6 us (0.968)
  Pallas kernels: 51.6 us -> 49.8 us
    pallas_call x1, Pallas kernels: 51.6 us -> 49.8 us  [local(): pl.pallas_call(kernel, out_shape=(jax.ShapeDtypeStruct((SLOT, QH * HD), B...]
where the time goes in v4:
time: 54.6 us; the launch traced here: 54.4 us
  Pallas kernels  49.8 us (91%)
  between operations  2.33 us (4%)
  local copies, waits for them, and re-layouts  2.29 us (4%)
    pallas_call x1, Pallas kernels, local(): pl.pallas_call(kernel, out_shape=(jax.ShapeDtypeStruct((SLOT, QH * HD), B...  49.8 us
    unnamed x1, local copies, waits for them, and re-layouts  2.29 us

profile of v4, /device:TPU:1, one launch (start us, length us, event | category | flops | bytes accessed | tf_op | source)
XLA Modules:
  0.0 54.4 jit_solution(11755357998025646240)
XLA Ops:
  0.6 49.8 %shard_map.95 = (bf16[128,4096]{1,0:T(8,128)(2,1)}, f32[1,1]{1,0:T(1,128)}) custom-call(bf16[128,4096]{1,0:T(8,128)(2,1)} %bitcast.9, bf16[256,512]{1,0:T(8,128)(2,1)} %bitcast.10, bf16[256,512]{1,0:T(8,128)(2,1)} %bitcast.11, bf16[128,512]{1,0:T(8,128)(2,1)} %bitcast.12, bf16[128,512]{1,0:T(8,128)(2,1)} %bitcast.13, s32[1,128]{1,0:T(1,128)} %slot_hbm.1, ...), custom_call_target="tpu_custom_call" | custom-call | flops 5400000000 | bytes 4000000 | tf_op jit(solution)/shard_map/pallas_call | solution.py:474
  50.4 2.3 %copy.12 = bf16[1,128,4096]{2,1,0:T(8,128)(2,1)} copy(bf16[1,128,4096]{2,1,0:T(8,128)(2,1)} %bitcast.8) | data formatting | bytes 2097152

commit v5 on v4

--- a/solution.py
+++ b/solution.py
@@ -58,7 +58,7 @@
         )
 
     column = [(0, 0, dz4, dc) for dz4 in range(4) for dc in range(2)][1:]
-    plane = [(dx, dy, 0, 0) for dx in range(4) for dy in range(NY)][1:]
+    plane = [(dx, dy, 0, 0) for dx in (2, 1, 3, 0) for dy in (2, 1, 3, 0)][:-1]
 
     def remote(src, dst, send, recv, target):
         return pltpu.make_async_remote_copy(
@@ -337,11 +337,13 @@
             for dy in ((2,), (1, 3))[n]
         ]
 
-    def far(i, carry):
-        plane = slice(2, 4)
-        keys = twice(jnp.concatenate([prompt(plane, 0), response(0)], axis=0))
-        values = with_ones(jnp.concatenate([prompt(plane, PKEYS), response(SLOT)], axis=0))
-        for j, s in enumerate(scores(0, i, keys)):
+    plane_keys = slice(2, 4)
+    keys = twice(jnp.concatenate([prompt(plane_keys, 0), response(0)], axis=0))
+    values = with_ones(jnp.concatenate([prompt(plane_keys, PKEYS), response(SLOT)], axis=0))
+    first = scores(0, 0, keys)
+    second = scores(0, 1, keys)
+    for i, ss in enumerate((first, second)):
+        for j, s in enumerate(ss):
             s = masked(0, s)
             at = pl.ds(i * 2 * HALF + j * HALF, HALF)
             before = top[at, :]
@@ -352,30 +354,22 @@
             finish(0, i, j, total)
         for copy in out_copies(0, i):
             copy.start()
-        return carry
-
-    lax.fori_loop(0, 2, far, 0)
-
-    def whole(i, carry):
-        for half in range(2):
-
-            @pl.when(i == half)
-            def _():
-                q_copies[1, half].wait_recv()
-                q_copies[3, half].wait_recv()
-                load_queries(1, half)
-
-        both = slice(0, 4)
-        keys = twice(jnp.concatenate([prompt(both, 0), response(0)], axis=0))
-        values = with_ones(jnp.concatenate([prompt(both, PKEYS), response(SLOT)], axis=0))
-        for j, s in enumerate(scores(1, i, keys)):
+
+    for half in range(2):
+        q_copies[1, half].wait_recv()
+        q_copies[3, half].wait_recv()
+        load_queries(1, half)
+    both = slice(0, 4)
+    keys = twice(jnp.concatenate([prompt(both, 0), response(0)], axis=0))
+    values = with_ones(jnp.concatenate([prompt(both, PKEYS), response(SLOT)], axis=0))
+    first = scores(1, 0, keys)
+    second = scores(1, 1, keys)
+    for i, ss in enumerate((first, second)):
+        for j, s in enumerate(ss):
             s = masked(1, s)
             finish(1, i, j, weigh(s, highest(s), values))
         for copy in out_copies(1, i):
             copy.start()
-        return carry
-
-    lax.fori_loop(0, 2, whole, 0)
 
     chosen = jnp.zeros((1, 1), F32)
     rejected = jnp.zeros((1, 1), F32)

time: 54.6 us -> 53.4 us (0.978)
  Pallas kernels: 49.8 us -> 48.6 us
    pallas_call x1, Pallas kernels: 49.8 us -> 48.6 us  [local(): pl.pallas_call(kernel, out_shape=(jax.ShapeDtypeStruct((SLOT, QH * HD), B...]
where the time goes in v5:
time: 53.4 us; the launch traced here: 53.2 us
  Pallas kernels  48.6 us (91%)
  between operations  2.33 us (4%)
  local copies, waits for them, and re-layouts  2.29 us (4%)
    pallas_call x1, Pallas kernels, local(): pl.pallas_call(kernel, out_shape=(jax.ShapeDtypeStruct((SLOT, QH * HD), B...  48.6 us
    unnamed x1, local copies, waits for them, and re-layouts  2.29 us

profile of v5, /device:TPU:1, one launch (start us, length us, event | category | flops | bytes accessed | tf_op | source)
XLA Modules:
  0.0 53.2 jit_solution(5571115337028358738)
XLA Ops:
  0.6 48.6 %shard_map.95 = (bf16[128,4096]{1,0:T(8,128)(2,1)}, f32[1,1]{1,0:T(1,128)}) custom-call(bf16[128,4096]{1,0:T(8,128)(2,1)} %bitcast.9, bf16[256,512]{1,0:T(8,128)(2,1)} %bitcast.10, bf16[256,512]{1,0:T(8,128)(2,1)} %bitcast.11, bf16[128,512]{1,0:T(8,128)(2,1)} %bitcast.12, bf16[128,512]{1,0:T(8,128)(2,1)} %bitcast.13, s32[1,128]{1,0:T(1,128)} %slot_hbm.1, ...), custom_call_target="tpu_custom_call" | custom-call | flops 5400000000 | bytes 4000000 | tf_op jit(solution)/shard_map/pallas_call | solution.py:468
  49.2 2.3 %copy.12 = bf16[1,128,4096]{2,1,0:T(8,128)(2,1)} copy(bf16[1,128,4096]{2,1,0:T(8,128)(2,1)} %bitcast.8) | data formatting | bytes 2097152

commit v6 on v5

--- a/solution.py
+++ b/solution.py
@@ -309,24 +309,30 @@
     lax.fori_loop(0, 2, near, 0)
 
     c_copies[NY].wait_recv()
-    for name in range(NY + 1):
-        zc_copies[name].wait_recv()
-
-    id_rows = [
-        row_ids(merged[g, j, RESP:, :].astype(F32)) for g in range(4) for j in range(2)
-    ]
     small[1].wait()
     small[2].wait()
     chosen_len = len_ref[:1, :1].astype(F32)
     rejected_len = len_ref[:1, 1:2].astype(F32)
+    seen = []
     for n in range(2):
         t = dot_t(eye, merged[0, firsts[n], RESP:, :])
         row_of = 32.0 * t[:, :1] + t[:, half_ids : half_ids + 1] - 32.0
-        lowest = jnp.where(row_of >= chosen_len, chosen_len, 0.0)
         qid[n] = jnp.broadcast_to(row_of, (SLOT, HD))
-        for m in range(8):
-            visible = (id_rows[m] <= row_of) & (id_rows[m] >= lowest)
-            bias[n, :, m * SLOT : (m + 1) * SLOT] = jnp.where(visible, HIGH, LOW)
+        seen.append((row_of, jnp.where(row_of >= chosen_len, chosen_len, 0.0)))
+
+    def mask(group):
+        for j in range(2):
+            row = row_ids(merged[group, j, RESP:, :].astype(F32))
+            at = slice((2 * group + j) * SLOT, (2 * group + j + 1) * SLOT)
+            for n, (row_of, lowest) in enumerate(seen):
+                visible = (row <= row_of) & (row >= lowest)
+                bias[n, :, at] = jnp.where(visible, HIGH, LOW)
+
+    for group in range(3):
+        mask(group)
+    for name in range(NY + 1):
+        zc_copies[name].wait_recv()
+    mask(3)
 
     def out_copies(n, i):
         return [

time: 53.4 us -> 53.2 us (level)
  no operation moved by 1% of the time
where the time goes in v6:
time: 53.2 us; the launch traced here: 53.1 us
  Pallas kernels  48.4 us (91%)
  between operations  2.33 us (4%)
  local copies, waits for them, and re-layouts  2.29 us (4%)
    pallas_call x1, Pallas kernels, local(): pl.pallas_call(kernel, out_shape=(jax.ShapeDtypeStruct((SLOT, QH * HD), B...  48.4 us
    unnamed x1, local copies, waits for them, and re-layouts  2.29 us

profile of v6, /device:TPU:1, one launch (start us, length us, event | category | flops | bytes accessed | tf_op | source)
XLA Modules:
  0.0 53.1 jit_solution(1431500522774026413)
XLA Ops:
  0.6 48.4 %shard_map.95 = (bf16[128,4096]{1,0:T(8,128)(2,1)}, f32[1,1]{1,0:T(1,128)}) custom-call(bf16[128,4096]{1,0:T(8,128)(2,1)} %bitcast.9, bf16[256,512]{1,0:T(8,128)(2,1)} %bitcast.10, bf16[256,512]{1,0:T(8,128)(2,1)} %bitcast.11, bf16[128,512]{1,0:T(8,128)(2,1)} %bitcast.12, bf16[128,512]{1,0:T(8,128)(2,1)} %bitcast.13, s32[1,128]{1,0:T(1,128)} %slot_hbm.1, ...), custom_call_target="tpu_custom_call" | custom-call | flops 5400000000 | bytes 4000000 | tf_op jit(solution)/shard_map/pallas_call | solution.py:474
  49.1 2.3 %copy.12 = bf16[1,128,4096]{2,1,0:T(8,128)(2,1)} copy(bf16[1,128,4096]{2,1,0:T(8,128)(2,1)} %bitcast.8) | data formatting | bytes 2097152
